TPU v7x, 128 devices: a whole 4x4x4 slice. The times are simulated.
128 devices in a mesh: seq: 16 (over y, z_lo, core), grp: 8 (over x, z_hi).
Axes of the slice: x: 4, y: 4, z: 4 (z_hi: 2, z_lo: 2; z = z_hi * 2 + z_lo), core: 2. Of those that a mesh axis runs over, the one named last changes fastest.
Arguments:
- tokens: bfloat16 [8, 4096, 768], P('grp', 'seq'), may hold values from -6 to 6
- sequence: int32 [8, 4096], P('grp'), may hold values from 0 to 4, as said below
- positions: int32 [8, 4096], P('grp'), may hold values from 0 to 2047, as said below
- first_gain: bfloat16 [768], replicated, may hold values from 0.5 to 1.5
- first_shift: bfloat16 [768], replicated, may hold values from -1.75 to 1.75
- input_weight: bfloat16 [768, 2304], replicated, may hold values from -0.21875 to 0.21875
- input_bias: bfloat16 [2304], replicated, may hold values from -1.75 to 1.75
- output_weight: bfloat16 [768, 768], replicated, may hold values from -3.5 to 3.5
- output_bias: bfloat16 [768], replicated, may hold values from -1.75 to 1.75
- second_gain: bfloat16 [768], replicated, may hold values from 0.5 to 1.5
- second_shift: bfloat16 [768], replicated, may hold values from -1.75 to 1.75
- up_weight: bfloat16 [768, 3072], replicated, may hold values from -0.21875 to 0.21875
- up_bias: bfloat16 [3072], replicated, may hold values from -1.75 to 1.75
- down_weight: bfloat16 [3072, 768], replicated, may hold values from -0.109375 to 0.109375
- down_bias: bfloat16 [768], replicated, may hold values from -1.75 to 1.75
- cotangent: bfloat16 [8, 4096, 768], P('grp', 'seq'), may hold values from -6 to 6
Outputs:
- result: bfloat16 [8, 4096, 768], P('grp', 'seq')
- grad_tokens: float32 [8, 4096, 768], P('grp', 'seq')
- grad_first_gain: float32 [768], replicated
- grad_first_shift: float32 [768], replicated
- grad_input_weight: float32 [768, 2304], replicated
- grad_input_bias: float32 [2304], replicated
- grad_output_weight: float32 [768, 768], replicated
- grad_output_bias: float32 [768], replicated
- grad_second_gain: float32 [768], replicated
- grad_second_shift: float32 [768], replicated
- grad_up_weight: float32 [768, 3072], replicated
- grad_up_bias: float32 [3072], replicated
- grad_down_weight: float32 [3072, 768], replicated
- grad_down_bias: float32 [768], replicated
Inputs may be any that keep to these rules, and one draw needn't show every extreme that they name: In each group id 0 marks one sequence of 2048 tokens and ids 1 upward sequences of 512 tokens; taken block by block in some order of the seq devices, the group's tokens are the sequences laid end to end in order of id; the first and the last device along seq hold tokens of sequence 0. Each sequence's tokens carry the positions 0 up to its length minus 1 in order.
All inputs are finite; a program needn't handle non-finite values.
Results may differ from a plain program's by a relative error of at most 0.0095.
Values may be sent and summed in bfloat16 or wider, within the bound.
No kernel may reach another device: no remote copies, remote signals or barrier semaphores. Data moves between devices by JAX's collectives and lax.ppermute only.
A program may use at most 320 MiB of HBM per device.

v0:
```python
import math

import jax
import jax.numpy as jnp
from jax import lax
from jax.sharding import PartitionSpec as P

H = 12
ROT = 16


EPS = 1e-05


def layer_norm(values, gain, shift):
    centre = values - jnp.mean(values, axis=-1, keepdims=True)
    spread = jnp.mean(centre * centre, axis=-1, keepdims=True)
    return centre * lax.rsqrt(spread + EPS) * gain + shift


def exact_gelu(values):
    return jax.nn.gelu(values, approximate=False)


def rotary_tables(places, width):
    half = width // 2
    freq = 1.0 / 10000.0 ** (jnp.arange(half, dtype=jnp.float32) * 2.0 / width)
    angle = places.astype(jnp.float32)[:, None] * freq[None, :]
    return (jnp.cos(angle)[:, None, :], jnp.sin(angle)[:, None, :])


def rotate(values, cosine, sine, width):
    half = width // 2
    first = values[..., :half]
    second = values[..., half:width]
    rest = values[..., width:]
    return jnp.concatenate(
        [first * cosine - second * sine, second * cosine + first * sine, rest], axis=-1
    )


def masked_probs(scores, visible):
    scores = jnp.where(visible, scores, -1e30)
    top = jnp.max(scores, axis=-1, keepdims=True)
    raised = jnp.exp(scores - top)
    return raised / jnp.sum(raised, axis=-1, keepdims=True)


def matmul(left, right):
    return jnp.dot(left, right, preferred_element_type=jnp.float32)


def inner_rows(left, right):
    return lax.dot_general(
        left, right, (((0,), (0,)), ((), ())), preferred_element_type=jnp.float32
    )


def times_transpose(left, right):
    return lax.dot_general(
        left, right, (((1,), (1,)), ((), ())), preferred_element_type=jnp.float32
    )


def head_major(rows, heads):
    return rows.reshape(rows.shape[0], heads, rows.shape[1] // heads).transpose(1, 0, 2)


def row_major(blocks):
    return blocks.transpose(1, 0, 2).reshape(blocks.shape[1], blocks.shape[0] * blocks.shape[2])


def turn_rows(rows, cosine, sine, heads):
    count = rows.shape[0]
    width = rows.shape[1]
    return rotate(rows.reshape(count, heads, width // heads), cosine, sine, ROT).reshape(
        count, width
    )


def body(
    tokens,
    sequence,
    positions,
    first_gain,
    first_shift,
    input_weight,
    input_bias,
    output_weight,
    output_bias,
    second_gain,
    second_shift,
    up_weight,
    up_bias,
    down_weight,
    down_bias,
    cotangent,
):
    count = tokens.shape[1]
    width = tokens.shape[2]
    heads = H
    score_scale = 1.0 / math.sqrt(width // heads)
    offset = lax.axis_index("seq") * count
    seq_all = sequence[0]
    place_all = positions[0]
    seq_own = lax.dynamic_slice_in_dim(seq_all, offset, count)
    place_own = lax.dynamic_slice_in_dim(place_all, offset, count)
    inputs = tokens[0].astype(jnp.float32)
    normed, first_back = jax.vjp(
        layer_norm, inputs, first_gain.astype(jnp.float32), first_shift.astype(jnp.float32)
    )
    normed_first = normed.astype(jnp.bfloat16)
    mixed = matmul(normed_first, input_weight) + input_bias.astype(jnp.float32)
    cosine, sine = rotary_tables(place_own, ROT)
    query_rows = turn_rows(mixed[:, :width], cosine, sine, heads).astype(jnp.bfloat16)
    key_rows = turn_rows(mixed[:, width : 2 * width], cosine, sine, heads).astype(jnp.bfloat16)
    value_rows = mixed[:, 2 * width :].astype(jnp.bfloat16)
    key_all, value_all = (
        lax.all_gather(key_rows, "seq", axis=0, tiled=True),
        lax.all_gather(value_rows, "seq", axis=0, tiled=True),
    )
    visible = (seq_own[:, None] == seq_all[None, :]) & (place_all[None, :] <= place_own[:, None])
    query_heads = head_major(query_rows, heads)
    key_heads = head_major(key_all, heads)
    value_heads = head_major(value_all, heads)

    def attend(operands):
        query_one, key_one, value_one = operands
        scores = score_scale * jnp.einsum(
            "qd,kd->qk", query_one, key_one, preferred_element_type=jnp.float32
        )
        weights = masked_probs(scores, visible)
        return jnp.einsum(
            "qk,kd->qd", weights.astype(jnp.bfloat16), value_one, preferred_element_type=jnp.float32
        )

    attended = row_major(lax.map(attend, (query_heads, key_heads, value_heads))).astype(
        jnp.bfloat16
    )
    attn_out = matmul(attended, output_weight) + output_bias.astype(jnp.float32)
    normed_two, second_back = jax.vjp(
        layer_norm, inputs, second_gain.astype(jnp.float32), second_shift.astype(jnp.float32)
    )
    normed_second = normed_two.astype(jnp.bfloat16)
    hidden_pre = matmul(normed_second, up_weight) + up_bias.astype(jnp.float32)
    activated, gelu_back = jax.vjp(exact_gelu, hidden_pre)
    activated_low = activated.astype(jnp.bfloat16)
    feed_out = matmul(activated_low, down_weight) + down_bias.astype(jnp.float32)
    result = (inputs + attn_out + feed_out).astype(jnp.bfloat16)[None]
    grad_rows = cotangent[0]
    grad_float = grad_rows.astype(jnp.float32)
    grad_down_weight = inner_rows(activated_low, grad_rows)
    grad_bias_sum = jnp.sum(grad_float, axis=0)
    grad_output_weight = inner_rows(attended, grad_rows)
    (grad_hidden,) = gelu_back(times_transpose(grad_rows, down_weight))
    grad_hidden_low = grad_hidden.astype(jnp.bfloat16)
    grad_up_weight = inner_rows(normed_second, grad_hidden_low)
    grad_up_bias = jnp.sum(grad_hidden_low.astype(jnp.float32), axis=0)
    grad_second_inputs, grad_second_gain, grad_second_shift = second_back(
        times_transpose(grad_hidden_low, up_weight)
    )
    grad_attended = times_transpose(grad_rows, output_weight).astype(jnp.bfloat16)
    grad_heads = head_major(grad_attended, heads)

    def attend_back(operands):
        query_one, key_one, value_one, grad_one = operands
        scores = score_scale * jnp.einsum(
            "qd,kd->qk", query_one, key_one, preferred_element_type=jnp.float32
        )
        weights = masked_probs(scores, visible)
        weights_low = weights.astype(jnp.bfloat16)
        grad_weights = jnp.einsum(
            "qd,kd->qk", grad_one, value_one, preferred_element_type=jnp.float32
        )
        row_total = jnp.sum(weights * grad_weights, axis=-1, keepdims=True)
        grad_scores = (weights * (grad_weights - row_total)).astype(jnp.bfloat16)
        grad_query = score_scale * jnp.einsum(
            "qk,kd->qd", grad_scores, key_one, preferred_element_type=jnp.float32
        )
        grad_key = score_scale * jnp.einsum(
            "qk,qd->kd", grad_scores, query_one, preferred_element_type=jnp.float32
        )
        grad_value = jnp.einsum(
            "qk,qd->kd", weights_low, grad_one, preferred_element_type=jnp.float32
        )
        return (grad_query, grad_key, grad_value)

    grad_query_heads, grad_key_heads, grad_value_heads = lax.map(
        attend_back, (query_heads, key_heads, value_heads, grad_heads)
    )
    key_terms = jnp.concatenate([row_major(grad_key_heads), row_major(grad_value_heads)], axis=1)
    key_share = lax.psum_scatter(key_terms, "seq", scatter_dimension=0, tiled=True)
    grad_key_rows = key_share[:, :width]
    grad_value_rows = key_share[:, width:]
    grad_query_rows = turn_rows(row_major(grad_query_heads), cosine, -sine, heads)
    grad_key_rows = turn_rows(grad_key_rows, cosine, -sine, heads)
    grad_mixed = jnp.concatenate([grad_query_rows, grad_key_rows, grad_value_rows], axis=1).astype(
        jnp.bfloat16
    )
    grad_input_weight = inner_rows(normed_first, grad_mixed)
    grad_input_bias = jnp.sum(grad_mixed.astype(jnp.float32), axis=0)
    grad_first_inputs, grad_first_gain, grad_first_shift = first_back(
        times_transpose(grad_mixed, input_weight)
    )
    grad_tokens = (grad_float + grad_first_inputs + grad_second_inputs)[None]
    (
        grad_first_gain,
        grad_first_shift,
        grad_input_weight,
        grad_input_bias,
        grad_output_weight,
        grad_bias_sum,
        grad_second_gain,
        grad_second_shift,
        grad_up_weight,
        grad_up_bias,
        grad_down_weight,
    ) = lax.psum(
        (
            grad_first_gain,
            grad_first_shift,
            grad_input_weight,
            grad_input_bias,
            grad_output_weight,
            grad_bias_sum,
            grad_second_gain,
            grad_second_shift,
            grad_up_weight,
            grad_up_bias,
            grad_down_weight,
        ),
        ("seq", "grp"),
    )
    return (
        result,
        grad_tokens,
        grad_first_gain,
        grad_first_shift,
        grad_input_weight,
        grad_input_bias,
        grad_output_weight,
        grad_bias_sum,
        grad_second_gain,
        grad_second_shift,
        grad_up_weight,
        grad_up_bias,
        grad_down_weight,
        grad_bias_sum,
    )


def solution(mesh):
    in_specs = (
        P("grp", "seq", None),
        P("grp", None),
        P("grp", None),
        P(),
        P(),
        P(),
        P(),
        P(),
        P(),
        P(),
        P(),
        P(),
        P(),
        P(),
        P(),
        P("grp", "seq", None),
    )
    out_specs = (
        P("grp", "seq", None),
        P("grp", "seq", None),
        P(),
        P(),
        P(),
        P(),
        P(),
        P(),
        P(),
        P(),
        P(),
        P(),
        P(),
        P(),
    )
    return jax.shard_map(body, mesh=mesh, in_specs=in_specs, out_specs=out_specs, check_vma=False)
```

profile of v0, /device:TPU:97, one launch (start us, length us, event | category | flops | bytes accessed | tf_op | source)
XLA Modules:
  0.0 891.1 jit_solution(875903899580124697)
XLA Ops:
  42.6 40.9 %all-gather.3.cloned.1.call-done = bf16[4096,768]{0,1:T(8,128)(2,1)} async-done(((bf16[256,768]{0,1:T(8,128)(2,1)}), bf16[4096,768]{0,1:T(8,128)(2,1)}) %all-gather.3.cloned.1.call-update) | async-done | bytes 6291472 | tf_op jit(solution)/shard_map/all_gather | solution.py:119
  83.5 12.1 %copy.45 = bf16[12,4096,64]{2,1,0:T(8,128)(2,1)} copy(bf16[12,4096,64]{1,2,0:T(8,128)(2,1)} %bitcast.237) | data formatting | bytes 12582912
  95.6 32.7 %all-gather.5.cloned.1.call-done = bf16[4096,768]{1,0:T(8,128)(2,1)} async-done(((bf16[256,768]{1,0:T(8,128)(2,1)}), bf16[4096,768]{1,0:T(8,128)(2,1)}) %all-gather.5.cloned.1.call-update) | async-done | bytes 6291472 | tf_op jit(solution)/shard_map/all_gather | solution.py:120
  128.3 8.6 copy.43
  136.9 12.0 %copy.46 = bf16[12,4096,64]{2,1,0:T(8,128)(2,1)} copy(bf16[12,4096,64]{1,2,0:T(8,128)(2,1)} %bitcast.233) | data formatting | bytes 12582912
  148.9 181.4 %while.29 = (s32[]{:T(128)}, f32[12,256,64]{1,2,0:T(8,128)}, f32[12,4096,64]{1,2,0:T(8,128)}, f32[12,4096,64]{1,2,0:T(8,128)}, bf16[12,256,64]{2,1,0:T(8,128)(2,...) while((s32[]{:T(128)}, f32[12,256,64]{1,2,0:T(8,128)}, ...), condition=%wide.region_10.11_spmd.clone.clone, body=%wide.region_6.10_spmd.clone.sunk.clone | while | flops 692337920 | bytes 41207924 | solution.py:188
  330.3 18.6 %pad_maximum_fusion = f32[4096,1536]{0,1:T(8,128)} fusion(f32[4096,768]{0,1:T(8,128)} %bitcast.234, f32[4096,768]{0,1:T(8,128)} %bitcast.24), kind=kLoop, calls=%fused_computation.54 | loop fusion | flops 6291456 | bytes 50331648 | tf_op jit(solution)/shard_map/concatenate | solution.py:191
  351.8 9.8 %multiply_convert_fusion.1 = (bf16[256,3072]{1,0:T(8,128)(2,1)S(1)}, f32[256,3072]{1,0:T(8,128)S(1)}, f32[256,3072]{1,0:T(8,128)S(1)}) fusion(f32[3072]{0:T(1024)S(1)} %convert_element_type.107, bf16[768,3072]{1,0:T(8,128)(2,1)} %param.31, bf16[1,256,768]{2,1,0:T(8,128)(2,1)} %param.20, f32[768]{0:T(1024)S(1)} %convert_element_type.105, ...), kind=kOutput, calls=%fused_computation.61 | convolution fusion | flops 1261043712 | bytes 12996608 | tf_op jit(solution)/shard_map/dot_general | solution.py:50
  361.6 5.2 fusion.79
  366.8 5.3 convert_reduce_fusion
  372.1 5.3 fusion.90
  379.2 73.0 %while.28 = (s32[]{:T(128)}, bf16[12,256,64]{1,2,0:T(8,128)(2,1)}, bf16[12,256,64]{2,1,0:T(8,128)(2,1)}, bf16[12,4096,64]{2,1,0:T(8,128)(2,1)}, bf16[12,4096,64]...) while((s32[]{:T(128)}, bf16[12,256,64]{1,2,0:T(8,128)(2,1)}, ...), condition=%wide.region_5.6_spmd.clone.clone, body=%wide.region_2.5_spmd.clone.sunk.clone | while | flops 279969280 | bytes 14853213 | solution.py:137
  382.4 2.9 fusion.155
  388.5 2.9 fusion.155
  394.6 2.9 fusion.155
  406.8 2.9 fusion.155
  419.0 2.9 fusion.155
  425.1 2.9 fusion.155
  431.2 2.9 fusion.155
  437.2 2.9 fusion.155
  443.3 2.9 fusion.155
  449.4 2.9 fusion.155
  452.2 3.0 fusion.81
  455.2 152.3 %reduce-scatter.2.cloned.1.call-done = f32[256,1536]{0,1:T(8,128)} async-done(((f32[4096,1536]{0,1:T(8,128)}), f32[256,1536]{0,1:T(8,128)}) %reduce-scatter.2.cloned.1.call-update) | async-done | bytes 1572880 | tf_op jit(solution)/shard_map/reduce_scatter | solution.py:192
  613.2 4.3 fusion.93
  618.8 4.3 fusion.105
  623.2 3.8 convolution_add_fusion.3
  635.6 73.5 %all-reduce = (f32[768]{0:T(1024)}, f32[768]{0:T(1024)}, f32[2304]{0:T(1024)}, f32[768]{0:T(1024)S(1)}, f32[768]{0:T(1024)}, /*index=5*/f32[768]{0:T(1024)}, f32[3072]{0:T(1024)}) all-reduce(f32[768]{0:T(1024)} %get-tuple-element.183, f32[768]{0:T(1024)} %get-tuple-element.180, ...), channel_id=1, replica_groups=mesh['seq'=16,'grp'=8] {'seq','grp'}, use_global_device_ids=true, to_apply=%region_17.18 | all-reduce | flops 9216 | bytes 73728 | tf_op jit(solution)/shard_map/psum | solution.py:218
  709.0 153.9 %all-reduce.4.cloned.1.call-done = (f32[768,2304]{1,0:T(8,128)}, f32[768,768]{1,0:T(8,128)}, f32[768,3072]{1,0:T(8,128)}, f32[3072,768]{1,0:T(8,128)}) async-done(((f32[768,2304]{1,0:T(8,128)}, f32[768,768]{1,0:T(8,128)}, f32[768,3072]{1,0:T(8,128)}, f32[3072,768]{1,0:T(8,128)}), (f32[768,2304]{1,0:T(8,128)}, f32[768,768]{1,0:T(8,128)}, f32[768,3072]{1,0:T(8,128)}, ...) | async-done | bytes 28311568 | tf_op jit(solution)/shard_map/psum | solution.py:218
  863.5 6.6 copy.82
  871.5 9.3 %copy.84 = f32[768,3072]{1,0:T(8,128)} copy(f32[768,3072]{1,0:T(8,128)} %get-tuple-element.567) | data formatting | bytes 18874368
  880.8 3.7 copy.85
  (240 shorter events, 282.6 us)
Async XLA Ops:
  7.2 5.4 copy-start
  7.2 76.3 %all-gather.3.cloned.1.call-start = ((), (), s32[]{:S(2)}) async-start(), calls=%async_computation.1 | async-start | bytes 6684672 | tf_op jit(solution)/shard_map/all_gather | solution.py:119
  10.4 4.3 copy-start.26
  10.5 361.6 %copy-start.23 = (f32[256]{0:T(256)}, f32[256]{0:T(256)S(1)}, u32[]{:S(2)}) copy-start(f32[256]{0:T(256)S(1)} %fusion.89) | copy-start | bytes 3076
  11.2 3.6 copy-start.18
  11.8 2.9 copy-start.20
  29.5 98.8 %all-gather.5.cloned.1.call-start = ((), (), s32[]{:S(2)}) async-start(), calls=%async_computation.2 | async-start | bytes 6684672 | tf_op jit(solution)/shard_map/all_gather | solution.py:120
  31.5 576.1 %reduce-scatter.2.cloned.1.call-start = ((), (), s32[]{:S(2)}) async-start(), calls=%async_computation.3 | async-start | bytes 26738688 | tf_op jit(solution)/shard_map/reduce_scatter | solution.py:192
  330.3 18.6 %copy-start.31 = (s32[256]{0:T(256)}, s32[256]{0:T(256)S(1)}, u32[]{:S(2)}) copy-start(s32[256]{0:T(256)S(1)} %get-tuple-element.604) | copy-start | bytes 3076
  348.9 514.0 %all-reduce.4.cloned.1.call-start = ((), (), s32[]{:S(2)}) async-start(), calls=%async_computation.4 | async-start | bytes 56623104 | tf_op jit(solution)/shard_map/psum | solution.py:218
  351.8 9.8 %copy-start.4 = (bf16[1,256,768]{2,1,0:T(8,128)(2,1)S(1)}, bf16[1,256,768]{2,1,0:T(8,128)(2,1)}, u32[]{:S(2)}) copy-start(bf16[1,256,768]{2,1,0:T(8,128)(2,1)} %param.35) | copy-start | bytes 1179652
  361.6 5.2 copy-start.13
  366.8 5.3 copy-start.1
  372.1 5.3 copy-start.17
  455.2 157.9 %copy-start.19 = (f32[768]{0:T(1024)S(1)}, f32[768]{0:T(1024)}, u32[]{:S(2)}) copy-start(f32[768]{0:T(1024)} %copy-done.18) | copy-start | bytes 9220
  455.2 157.9 %copy-start.21 = (f32[768]{0:T(1024)S(1)}, f32[768]{0:T(1024)}, u32[]{:S(2)}) copy-start(f32[768]{0:T(1024)} %copy-done.20) | copy-start | bytes 9220
  607.6 5.6 copy-start.2
  607.6 5.6 copy-start.24
  618.8 4.4 copy-start.14
  623.2 3.9 copy-start.3
  623.2 3.9 copy-start.6
  627.1 2.4 copy-start.8
  627.1 2.4 copy-start.10
  627.1 2.4 copy-start.12
  630.5 1.9 copy-start.27
  630.5 1.9 copy-start.25
  630.5 3.1 copy-start.5
  709.0 161.1 %copy-start.28 = (f32[768]{0:T(1024)}, f32[768]{0:T(1024)S(1)}, u32[]{:S(2)}) copy-start(f32[768]{0:T(1024)S(1)} %get-tuple-element.564) | copy-start | bytes 9220
  863.5 6.6 copy-start.15
  870.1 10.7 %slice-start = ((s8[9437184]{0:T(1024)(128)(4,1)}), s8[4194304]{0:T(1024)(128)(4,1)S(1)}, s32[]{:S(2)}) async-start(s8[9437184]{0:T(1024)(128)(4,1)} %bitcast.235), calls=%async_computation.5 | async-start | bytes 8388608
  871.5 9.3 %slice-start.1 = ((s8[9437184]{0:T(1024)(128)(4,1)}), s8[4194304]{0:T(1024)(128)(4,1)S(1)}, s32[]{:S(2)}) async-start(s8[9437184]{0:T(1024)(128)(4,1)} %bitcast.235), calls=%async_computation.6 | async-start | bytes 8388608
  871.5 9.3 %slice-start.2 = ((s8[9437184]{0:T(1024)(128)(4,1)}), s8[1048576]{0:T(1024)(128)(4,1)S(1)}, s32[]{:S(2)}) async-start(s8[9437184]{0:T(1024)(128)(4,1)} %bitcast.235), calls=%async_computation.7 | async-start | bytes 2097152
  (7 other events, 7.1 us)
Sparse Core Ops, SparseCore 0:
  29.6 53.8 all-gather.2
  85.8 42.4 all-gather.4
  349.1 258.4 reduce-scatter.1
  617.6 245.2 all-reduce.3
where the time goes:
time: 899 us; the launch traced here: 891 us
  waiting for transfers between devices  380 us (42%)
  matrix products  268 us (30%)
  local copies, waits for them, and re-layouts  79.5 us (9%)
  other arithmetic  76 us (8%)
  blocking collectives  73.5 us (8%)
  between operations  14.1 us (2%)
    psum x1, waiting for transfers between devices, body(): lax.psum((grad_first_gain, grad_first_shift, grad_input_weight, grad_inpu...  154 us
    reduce_scatter x1, waiting for transfers between devices, body(): lax.psum_scatter(key_terms, 'seq', scatter_dimension=0, tiled=True)  152 us
    psum x1, blocking collectives, body(): lax.psum((grad_first_gain, grad_first_shift, grad_input_weight, grad_inpu...  73.5 us
    unnamed x78, local copies, waits for them, and re-layouts  51.8 us
    all_gather x1, waiting for transfers between devices, body(): lax.all_gather(key_rows, 'seq', axis=0, tiled=True)  40.9 us
    dot_general x12, matrix products, attend(): jnp.einsum('qk,kd->qd', weights.astype(jnp.bfloat16), value_one, preferre...  34.6 us
    all_gather x1, waiting for transfers between devices, body(): lax.all_gather(value_rows, 'seq', axis=0, tiled=True)  32.7 us
    dot_general x12, matrix products, attend_back(): jnp.einsum('qk,qd->kd', weights_low, grad_one, preferred_element_type=jnp...  32.1 us
  transfers between devices with their start and end apart: 4, of which 4 were waited for; matrix products, arithmetic and copies ran while one was open for 17% of the time, Pallas kernels for 0%

commit v1 on v0

v1 whole, which is shorter than its diff:
```python
import math

import jax
import jax.numpy as jnp
import numpy as np
from jax import lax
from jax.experimental import pallas as pl
from jax.experimental.pallas import tpu as pltpu
from jax.sharding import PartitionSpec as P

H = 12
DH = 64
D = 768
FF = 3072
ROT = 16
TOK = 256
SEQ_DEV = 16
LONG_BLOCKS = 8
EPS = 1e-05
F32 = jnp.float32
BF16 = jnp.bfloat16
TILE = 512


def place(index):
    seq, grp = index // 8, index % 8
    return {
        "x": grp // 2,
        "y": seq // 4,
        "z": (grp % 2) * 2 + (seq // 2) % 2,
        "c": seq % 2,
    }


def index_of(at):
    seq = at["y"] * 4 + (at["z"] % 2) * 2 + at["c"]
    grp = at["x"] * 2 + at["z"] // 2
    return seq * 8 + grp


def swap(value, partner):
    pairs = [(i, index_of(partner(place(i)))) for i in range(128)]
    return lax.ppermute(value, ("seq", "grp"), pairs)


def here():
    seq, grp = lax.axis_index("seq"), lax.axis_index("grp")
    return {
        "x": grp // 2,
        "y": seq // 4,
        "z": (grp % 2) * 2 + (seq // 2) % 2,
        "c": seq % 2,
    }


def other_core(at):
    return {**at, "c": 1 - at["c"]}


def ring_partner(axis, step):
    def partner(at):
        i = at[axis]
        return {**at, axis: i ^ 1 if step == at["c"] else 3 - i}

    return partner


def ring_bits(i, core):
    inner = ((i == 1) | (i == 2)).astype(jnp.int32)
    upper = (i >= 2).astype(jnp.int32)
    return jnp.where(core == 0, inner, upper), jnp.where(core == 0, upper, inner)


def half(value, which):
    rows = value.shape[0] // 2
    return lax.dynamic_slice_in_dim(value, which * rows, rows, 0)


def ring_scatter(value, axis, at):
    for step, bit in enumerate(ring_bits(at[axis], at["c"])):
        got = swap(half(value, 1 - bit), ring_partner(axis, step))
        value = (half(value, bit).astype(F32) + got.astype(F32)).astype(BF16)
    return value


def ring_gather(value, axis, at, ordered):
    bits = ring_bits(at[axis], at["c"])
    for step in (1, 0):
        got = swap(value, ring_partner(axis, step))
        if ordered:
            first = jnp.where(bits[step] == 0, value, got)
            second = jnp.where(bits[step] == 0, got, value)
            value = jnp.concatenate([first, second], 0)
        else:
            value = jnp.concatenate([value, got], 0)
    return value


def contract(left, right, dims):
    return lax.dot_general(left, right, (dims, ((), ())), preferred_element_type=F32)


def rotate_rows(rows, cosine, sine):
    first, second = rows[0:8], rows[8:16]
    return jnp.concatenate(
        [first * cosine - second * sine, second * cosine + first * sine, rows[16:]], 0
    )


def head_kernel(
    logical, place_block, live,
    rows_ref, table_ref, w_ref, wo_ref, bias_ref, norm_ref, extra_ref,
    send_ref, grad_ref,
    t_ref, q_ref, k_ref, v_ref, g_ref, s_ref, p_ref, dk_ref, dv_ref, o_ref, gw_ref, go_ref, gb_ref, gc_ref,
):
    def project(b, _):
        at = pl.multiple_of(b * TOK, TOK)
        to = pl.multiple_of(logical[b] * TOK, TOK)
        pos = pl.multiple_of(place_block[b] * TOK, TOK)
        cosine = table_ref[0:8, pl.ds(pos, TOK)]
        sine = table_ref[8:16, pl.ds(pos, TOK)]
        mixed = contract(w_ref[...], rows_ref[pl.ds(at, TOK), 0:D], ((1,), (1,)))
        mixed = mixed + bias_ref[:, 0:1]
        query = rotate_rows(mixed[0:64], cosine, sine) * 0.125
        key = rotate_rows(mixed[64:128], cosine, sine)
        value = mixed[128:192]
        grad = contract(wo_ref[...], rows_ref[pl.ds(at, TOK), D:], ((1,), (1,)))
        for n, (part, ref) in enumerate(
            ((query, q_ref), (key, k_ref), (value, v_ref), (grad, g_ref))
        ):
            t_ref[n * 64 : n * 64 + 64, pl.ds(to, TOK)] = part.astype(BF16)
            ref[pl.ds(to, TOK), :] = part.T.astype(BF16)
        return 0

    lax.fori_loop(0, SEQ_DEV, project, 0)
    dk_ref[...] = jnp.zeros_like(dk_ref)
    dv_ref[...] = jnp.zeros_like(dv_ref)

    def attend(task, _):
        base = pl.multiple_of(task * TILE, TILE)
        full = jnp.where(task < 4, task, 0)
        q_t = t_ref[0:64, pl.ds(base, TILE)]
        g_t = t_ref[192:256, pl.ds(base, TILE)]

        def score(keys, slot, top, masked):
            scores = contract(k_ref[pl.ds(keys, TILE), :], q_t, ((1,), (0,)))
            if masked:
                key_at = lax.broadcasted_iota(jnp.int32, (TILE, TILE), 0)
                query_at = lax.broadcasted_iota(jnp.int32, (TILE, TILE), 1)
                scores = jnp.where(key_at <= query_at, scores, -1e30)
            s_ref[pl.ds(slot, TILE), :] = scores
            return jnp.maximum(top, jnp.max(scores, axis=0, keepdims=True))

        last = pl.multiple_of(full * TILE, TILE)
        top = score(base, last, jnp.full((1, TILE), -1e30, F32), True)

        def score_step(j, top):
            at = pl.multiple_of(j * TILE, TILE)
            return score(at, at, top, False)

        top = lax.fori_loop(0, full, score_step, top)

        def weigh(keys, slot, carry):
            total, dot_total, out = carry
            raised = jnp.exp(s_ref[pl.ds(slot, TILE), :] - top)
            s_ref[pl.ds(slot, TILE), :] = raised
            grads = contract(v_ref[pl.ds(keys, TILE), :], g_t, ((1,), (0,)))
            p_ref[pl.ds(slot, TILE), :] = grads
            total = total + jnp.sum(raised, axis=0, keepdims=True)
            dot_total = dot_total + jnp.sum(raised * grads, axis=0, keepdims=True)
            out = out + contract(
                t_ref[128:192, pl.ds(keys, TILE)], raised.astype(BF16), ((1,), (0,))
            )
            return total, dot_total, out

        carry = (jnp.zeros((1, TILE), F32), jnp.zeros((1, TILE), F32), jnp.zeros((64, TILE), F32))
        carry = weigh(base, last, carry)

        def weigh_step(j, carry):
            at = pl.multiple_of(j * TILE, TILE)
            return weigh(at, at, carry)

        total, dot_total, out = lax.fori_loop(0, full, weigh_step, carry)
        scale = 1.0 / total
        row_total = dot_total * scale
        o_ref[0:64, pl.ds(base, TILE)] = (out * scale).astype(BF16)

        def back(keys, slot, grad_q):
            probs = s_ref[pl.ds(slot, TILE), :] * scale
            grads = probs * (p_ref[pl.ds(slot, TILE), :] - row_total)
            grads = grads.astype(BF16)
            dv_ref[pl.ds(keys, TILE), :] += contract(
                probs.astype(BF16), g_ref[pl.ds(base, TILE), :], ((1,), (0,))
            )
            dk_ref[pl.ds(keys, TILE), :] += contract(
                grads, q_ref[pl.ds(base, TILE), :], ((1,), (0,))
            )
            return grad_q + contract(t_ref[64:128, pl.ds(keys, TILE)], grads, ((1,), (0,)))

        grad_q = back(base, last, jnp.zeros((64, TILE), F32))

        def back_step(j, grad_q):
            at = pl.multiple_of(j * TILE, TILE)
            return back(at, at, grad_q)

        grad_q = lax.fori_loop(0, full, back_step, grad_q) * 0.125
        cosine = table_ref[0:8, pl.ds(last, TILE)]
        sine = table_ref[8:16, pl.ds(last, TILE)]
        o_ref[64:128, pl.ds(base, TILE)] = rotate_rows(grad_q, cosine, -sine).astype(BF16)
        return 0

    lax.fori_loop(0, 8, attend, 0)

    def turn_back(task, _):
        base = pl.multiple_of(task * TILE, TILE)
        pos = pl.multiple_of(jnp.where(task < 4, task, 0) * TILE, TILE)
        cosine = table_ref[0:8, pl.ds(pos, TILE)]
        sine = table_ref[8:16, pl.ds(pos, TILE)]
        grad_k = dk_ref[pl.ds(base, TILE), :].T
        o_ref[128:192, pl.ds(base, TILE)] = rotate_rows(grad_k, cosine, -sine).astype(BF16)
        o_ref[192:256, pl.ds(base, TILE)] = dv_ref[pl.ds(base, TILE), :].T.astype(BF16)
        return 0

    lax.fori_loop(0, 8, turn_back, 0)
    gw_ref[...] = jnp.zeros_like(gw_ref)
    go_ref[...] = jnp.zeros_like(go_ref)
    gb_ref[...] = jnp.zeros_like(gb_ref)
    gc_ref[...] = jnp.zeros_like(gc_ref)

    def collect(b, _):
        at = pl.multiple_of(b * TOK, TOK)
        frm = pl.multiple_of(logical[b] * TOK, TOK)
        block = o_ref[:, pl.ds(frm, TOK)]
        send_ref[b] = block
        grads = block[64:256]
        gw_ref[...] += contract(grads, rows_ref[pl.ds(at, TOK), 0:D], ((1,), (0,)))
        go_ref[...] += contract(block[0:64], rows_ref[pl.ds(at, TOK), D:], ((1,), (0,)))
        gb_ref[...] += contract(jnp.ones((8, TOK), BF16), grads, ((1,), (1,)))
        gc_ref[...] += jnp.broadcast_to(
            jnp.sum(grads.astype(F32), axis=1, keepdims=True), (192, 128)
        )
        return 0

    lax.fori_loop(0, SEQ_DEV, collect, 0)
    grad_ref[0:192, :] = gw_ref[...].astype(BF16)
    grad_ref[192:256, :] = go_ref[...].astype(BF16)
    alive = live[0].astype(F32)
    weights = w_ref[...].astype(F32)
    sums = gc_ref[:, 0:1]
    shift_grad = jnp.sum(sums * weights, axis=0, keepdims=True) * alive
    gain_grad = jnp.sum(
        weights * (gw_ref[...] - sums * norm_ref[1:2, :]), axis=0, keepdims=True
    ) * alive / norm_ref[0:1, :]
    bias_row = jnp.concatenate([gb_ref[0:1, :], jnp.zeros((1, D - 192), F32)], 1) * alive
    grad_ref[256:272, :] = jnp.concatenate(
        [gain_grad, shift_grad, bias_row, jnp.zeros((5, D), F32), extra_ref[...]], 0
    ).astype(BF16)


def one_head(logical, place_block, live, rows, table, w_t, wo, bias, norm, extra):
    count = SEQ_DEV * TOK
    vmem = pl.BlockSpec(memory_space=pltpu.VMEM)
    return pl.pallas_call(
        head_kernel,
        out_shape=(
            jax.ShapeDtypeStruct((SEQ_DEV, 256, TOK), BF16),
            jax.ShapeDtypeStruct((272, D), BF16),
        ),
        grid_spec=pltpu.PrefetchScalarGridSpec(
            num_scalar_prefetch=3,
            grid=(),
            in_specs=[vmem] * 7,
            out_specs=(vmem, vmem),
            scratch_shapes=[
                pltpu.VMEM((256, count), BF16),
                pltpu.VMEM((count, DH), BF16),
                pltpu.VMEM((count, DH), BF16),
                pltpu.VMEM((count, DH), BF16),
                pltpu.VMEM((count, DH), BF16),
                pltpu.VMEM((4 * TILE, TILE), F32),
                pltpu.VMEM((4 * TILE, TILE), F32),
                pltpu.VMEM((count, DH), F32),
                pltpu.VMEM((count, DH), F32),
                pltpu.VMEM((256, count), BF16),
                pltpu.VMEM((192, D), F32),
                pltpu.VMEM((64, D), F32),
                pltpu.VMEM((8, 192), F32),
                pltpu.VMEM((192, 128), F32),
            ],
        ),
        compiler_params=pltpu.CompilerParams(vmem_limit_bytes=56 * 2**20),
        cost_estimate=pl.CostEstimate(
            flops=40 * 10**9, bytes_accessed=16 * 10**6, transcendentals=4 * 10**6
        ),
    )(logical, place_block, live, rows, table, w_t, wo, bias, norm, extra)


def rotary_table():
    freq = (1.0 / 10000.0 ** (np.arange(8, dtype=np.float64) * 2.0 / ROT)).astype(np.float32)
    angle = np.arange(2048, dtype=np.float32)[None, :] * freq[:, None]
    angle = angle.astype(np.float64)
    return np.concatenate([np.cos(angle), np.sin(angle)], 0).astype(np.float32)


def place_feed_kernel(own_chunk, mine_ref, theirs_ref, down_ref, up_ref):
    def put(block):
        down_ref[...] = block[:, 0:D].astype(F32)
        up_ref[...] = block[:, D:].astype(F32).T

    step = pl.program_id(0)

    @pl.when(step < 4)
    def _():
        put(mine_ref[...])

    @pl.when(step >= 4)
    def _():
        put(theirs_ref[...])


def place_feed(own_chunk, mine, theirs):
    rows = FF // 8

    def spot(step, where):
        own = step < 4
        core = jnp.where(own, where[2], 1 - where[2])
        chunk = jnp.where(own, where[0], where[1])
        return core * 4 + ((step % 4) ^ chunk)

    return pl.pallas_call(
        place_feed_kernel,
        out_shape=(
            jax.ShapeDtypeStruct((FF, D), F32),
            jax.ShapeDtypeStruct((D, FF), F32),
        ),
        grid_spec=pltpu.PrefetchScalarGridSpec(
            num_scalar_prefetch=1,
            grid=(8,),
            in_specs=[
                pl.BlockSpec((rows, 2 * D), lambda s, w: (jnp.minimum(s, 3), 0)),
                pl.BlockSpec((rows, 2 * D), lambda s, w: (jnp.maximum(s - 4, 0), 0)),
            ],
            out_specs=(
                pl.BlockSpec((rows, D), lambda s, w: (spot(s, w), 0)),
                pl.BlockSpec((D, rows), lambda s, w: (0, spot(s, w))),
            ),
        ),
        compiler_params=pltpu.CompilerParams(vmem_limit_bytes=40 * 2**20),
        cost_estimate=pl.CostEstimate(flops=0, bytes_accessed=28 * 10**6, transcendentals=0),
    )(own_chunk, mine, theirs)


def norm_parts(values):
    centre = values - jnp.mean(values, axis=-1, keepdims=True)
    spread = jnp.mean(centre * centre, axis=-1, keepdims=True)
    rate = lax.rsqrt(spread + EPS)
    return centre * rate, rate


def norm_back(normal, rate, grad, gain):
    scaled = grad * gain
    return rate * (
        scaled
        - jnp.mean(scaled, axis=-1, keepdims=True)
        - normal * jnp.mean(scaled * normal, axis=-1, keepdims=True)
    )


def gelu_and_slope(values):
    cdf = 0.5 * (1.0 + lax.erf(values * np.float32(math.sqrt(0.5))))
    pdf = jnp.exp(-0.5 * values * values) * np.float32(1.0 / math.sqrt(2.0 * math.pi))
    return values * cdf, cdf + values * pdf


def body(
    tokens,
    sequence,
    positions,
    first_gain,
    first_shift,
    input_weight,
    input_bias,
    output_weight,
    output_bias,
    second_gain,
    second_shift,
    up_weight,
    up_bias,
    down_weight,
    down_bias,
    cotangent,
):
    at = here()
    seq = lax.axis_index("seq")
    core = at["c"]
    inputs = tokens[0].astype(F32)
    grad_rows = cotangent[0]
    grad_float = grad_rows.astype(F32)
    gain_one, shift_one = first_gain.astype(F32), first_shift.astype(F32)
    gain_two, shift_two = second_gain.astype(F32), second_shift.astype(F32)
    normal, rate = norm_parts(inputs)
    normed_first = (normal * gain_one + shift_one).astype(BF16)
    normed_second = (normal * gain_two + shift_two).astype(BF16)

    with jax.named_scope("gather_rows"):
        rows_all = lax.all_gather(
            jnp.concatenate([normed_first, grad_rows], 1), "seq", axis=0, tiled=True
        )

    with jax.named_scope("feed"):
        own = jnp.concatenate([normed_second, grad_rows], 1)
        both = jnp.concatenate([own, swap(own, other_core)], 0)
        units = FF // 2
        up_half = lax.dynamic_slice_in_dim(up_weight, core * units, units, 1)
        down_half = lax.dynamic_slice_in_dim(down_weight, core * units, units, 0)
        bias_half = lax.dynamic_slice_in_dim(up_bias, core * units, units, 0).astype(F32)
        second_both, grad_both = both[:, :D], both[:, D:]
        hidden = contract(second_both, up_half, ((1,), (0,))) + bias_half
        active, slope = gelu_and_slope(hidden)
        active = active.astype(BF16)
        grad_hidden = (contract(grad_both, down_half, ((1,), (1,))) * slope).astype(BF16)
        grad_down = contract(active, grad_both, ((0,), (0,))).astype(BF16)
        grad_up = contract(grad_hidden, second_both, ((0,), (0,))).astype(BF16)
        feed_sum = jnp.concatenate([grad_down, grad_up], 1)
        up_bias_part = jnp.sum(grad_hidden.astype(F32), axis=0)
        feed_part = contract(active, down_half, ((1,), (0,)))
        back_part = contract(grad_hidden, up_half, ((1,), (1,)))
        parts = jnp.concatenate([feed_part, back_part], 1)
        got = swap(parts[TOK:].astype(BF16), other_core).astype(F32)
        parts = parts[:TOK] + got
        feed_out = parts[:, :D] + down_bias.astype(F32)
        grad_second = parts[:, D:]
        grad_second_inputs = norm_back(normal, rate, grad_second, gain_two)
        extra = jnp.concatenate(
            [
                jnp.sum(grad_float, axis=0)[None],
                jnp.sum(grad_second * normal, axis=0)[None],
                jnp.sum(grad_second, axis=0)[None],
                up_bias_part.reshape(2, D),
                jnp.zeros((3, D), F32),
            ],
            0,
        )

    with jax.named_scope("feed_scatter"):
        for axis in ("x", "y", "z"):
            feed_sum = ring_scatter(feed_sum, axis, at)

    with jax.named_scope("head"):
        starts = jnp.arange(SEQ_DEV) * TOK
        ids, places = sequence[0][starts], positions[0][starts] // TOK
        logical = jnp.where(ids == 0, places, LONG_BLOCKS + 2 * (ids - 1) + places)
        head = jnp.minimum(seq, H - 1)
        live = (seq < H).astype(jnp.int32)[None]
        cut = [
            lax.dynamic_slice_in_dim(input_weight, n * D + head * DH, DH, 1) for n in range(3)
        ]
        cut_bias = [
            lax.dynamic_slice_in_dim(input_bias, n * D + head * DH, DH, 0) for n in range(3)
        ]
        w_t = jnp.concatenate(cut, 1).T
        bias = jnp.broadcast_to(jnp.concatenate(cut_bias).astype(F32)[:, None], (192, 128))
        wo = lax.dynamic_slice_in_dim(output_weight, head * DH, DH, 0)
        norm = jnp.concatenate([gain_one[None], shift_one[None], jnp.zeros((6, D), F32)], 0)
        send, head_sum = one_head(
            logical.astype(jnp.int32),
            places.astype(jnp.int32),
            live,
            rows_all,
            jnp.asarray(rotary_table()),
            w_t,
            wo,
            bias,
            norm,
            extra,
        )

    with jax.named_scope("head_sum"):
        for partner in (
            ring_partner("x", 0),
            ring_partner("x", 1),
            lambda p: {**p, "z": p["z"] ^ 2},
        ):
            got = swap(head_sum, partner)
            head_sum = (head_sum.astype(F32) + got.astype(F32)).astype(BF16)
        sums = lax.all_gather(head_sum, "seq", axis=0)

    with jax.named_scope("heads_back"):
        got = lax.all_to_all(send, "seq", 0, 0, tiled=True)[:H]
        attended = got[:, 0:64].reshape(D, TOK)
        grad_mixed = got[:, 64:].reshape(H, 3, DH, TOK).transpose(1, 0, 2, 3).reshape(3 * D, TOK)
        attn_out = contract(attended, output_weight, ((0,), (0,))) + output_bias.astype(F32)
        result = (inputs + attn_out + feed_out).astype(BF16)[None]
        grad_first = contract(grad_mixed, input_weight, ((0,), (1,)))
        grad_first_inputs = norm_back(normal, rate, grad_first, gain_one)
        grad_tokens = (grad_float + grad_first_inputs + grad_second_inputs)[None]

    with jax.named_scope("feed_gather"):
        for axis, ordered in (("z", True), ("y", True), ("x", False)):
            feed_sum = ring_gather(feed_sum, axis, at, ordered)
        theirs = swap(feed_sum, other_core)
        chunks = []
        for which in (core, 1 - core):
            first, second = ring_bits(at["x"], which)
            chunks.append(first * 2 + second)
        where = jnp.stack([*chunks, core]).astype(jnp.int32)
        grad_down_weight, grad_up_weight = place_feed(where, feed_sum, theirs)

    with jax.named_scope("head_place"):
        heads = sums[:H].astype(F32)
        grad_input_weight = (
            heads[:, 0:192].reshape(H, 3, DH, D).transpose(3, 1, 0, 2).reshape(D, 3 * D)
        )
        grad_output_weight = heads[:, 192:256].reshape(D, D)
        rest = sums[:, 256:].astype(F32)
        grad_input_bias = (
            rest[:H, 2, :192].reshape(H, 3, DH).transpose(1, 0, 2).reshape(3 * D)
        )
        added = jnp.sum(rest, axis=0)
        up_rows = jnp.sum(rest[:, 11:13].reshape(SEQ_DEV // 2, 2, 2 * D), axis=0)
        grad_up_bias = up_rows.reshape(FF)
    return (
        result,
        grad_tokens,
        added[0],
        added[1],
        grad_input_weight,
        grad_input_bias,
        grad_output_weight,
        added[8],
        added[9],
        added[10],
        grad_up_weight,
        grad_up_bias,
        grad_down_weight,
        added[8],
    )


def solution(mesh):
    split = P("grp", "seq", None)
    in_specs = (split, P("grp", None), P("grp", None), *(P(),) * 12, split)
    out_specs = (split, split, *(P(),) * 12)
    return jax.shard_map(body, mesh=mesh, in_specs=in_specs, out_specs=out_specs, check_vma=False)
```

time: 899 us -> 362 us (0.40)
  matrix products: 268 us -> 15.8 us
  waiting for transfers between devices: 380 us -> 151 us
  blocking collectives: 73.5 us -> 0 us
  starting transfers between devices: 0.34 us -> 60.8 us
  Pallas kernels: 0 us -> 50.4 us
  other arithmetic: 76 us -> 30 us
  local copies, waits for them, and re-layouts: 79.5 us -> 37.8 us
    dot_general x96 -> x8, matrix products: 268 us -> 15.8 us  [contract(): lax.dot_general(left, right, (dims, ((), ())), preferred_element_type=F32)]
    psum x1 -> x0, waiting for transfers between devices: 154 us -> none  [body(): lax.psum((grad_first_gain, grad_first_shift, grad_input_weight, grad_inpu...]
    reduce_scatter x1 -> x0, waiting for transfers between devices: 152 us -> none  [body(): lax.psum_scatter(key_terms, 'seq', scatter_dimension=0, tiled=True)]
    ppermute x0 -> x18, waiting for transfers between devices: none -> 135 us  [swap(): return lax.ppermute(value, ('seq', 'grp'), pairs)]
    all_gather x2, waiting for transfers between devices: 73.6 us -> 0.02 us  [the longest x1 0.02 us: body(): lax.all_gather(jnp.concatenate([normed_first, grad_rows], 1), 'seq', axis...]
    psum x1 -> x0, blocking collectives: 73.5 us -> none  [body(): lax.psum((grad_first_gain, grad_first_shift, grad_input_weight, grad_inpu...]
    pallas_call x0 -> x2, Pallas kernels: none -> 50.4 us  [the longest x1 37.6 us: one_head(): pl.pallas_call(head_kernel, out_shape=(jax.ShapeDtypeStruct((SEQ_DEV, 256...]
    ppermute x0 -> x18, starting transfers between devices: none -> 44.6 us  [swap(): return lax.ppermute(value, ('seq', 'grp'), pairs)]
  transfers between devices with their start and end apart: 4 -> 21, of which waited for: 4 -> 14; matrix products, arithmetic and copies ran while one was open for 17% -> 9% of each run, Pallas kernels for 0% -> 14%
where the time goes in v1:
time: 362 us; the launch traced here: 361 us
  waiting for transfers between devices  151 us (42%)
  starting transfers between devices  60.8 us (17%)
  Pallas kernels  50.4 us (14%)
  local copies, waits for them, and re-layouts  37.8 us (10%)
  other arithmetic  30 us (8%)
  matrix products  15.8 us (4%)
  between operations  14.7 us (4%)
    ppermute x18, waiting for transfers between devices, swap(): return lax.ppermute(value, ('seq', 'grp'), pairs)  135 us
    ppermute x18, starting transfers between devices, swap(): return lax.ppermute(value, ('seq', 'grp'), pairs)  44.6 us
    pallas_call x1, Pallas kernels, one_head(): pl.pallas_call(head_kernel, out_shape=(jax.ShapeDtypeStruct((SEQ_DEV, 256...  37.6 us
    all_to_all x1, starting transfers between devices, body(): got = lax.all_to_all(send, 'seq', 0, 0, tiled=True)[:H]  16.2 us
    dot_general x8, matrix products, contract(): lax.dot_general(left, right, (dims, ((), ())), preferred_element_type=F32)  15.8 us
    all_to_all x1, waiting for transfers between devices, body(): got = lax.all_to_all(send, 'seq', 0, 0, tiled=True)[:H]  15.8 us
    pallas_call x1, Pallas kernels, place_feed(): pl.pallas_call(place_feed_kernel, out_shape=(jax.ShapeDtypeStruct((FF, D)...  12.8 us
    unnamed x67, local copies, waits for them, and re-layouts  12.5 us
  transfers between devices with their start and end apart: 21, of which 14 were waited for; matrix products, arithmetic and copies ran while one was open for 9% of the time, Pallas kernels for 14%

profile of v1, /device:TPU:97, one launch (start us, length us, event | category | flops | bytes accessed | tf_op | source)
XLA Modules:
  0.0 360.8 jit_solution(10350870673635371894)
XLA Ops:
  14.3 2.0 collective-permute-done
  17.5 3.2 multiply_convert_fusion
  20.8 2.8 convert_reduce_fusion
  32.5 2.9 convolution_convert_fusion
  39.1 2.5 collective-permute-start.5
  41.6 26.7 %collective-permute-done.5 = bf16[768,1536]{1,0:T(8,128)(2,1)} collective-permute-done((bf16[768,1536]{1,0:T(8,128)(2,1)}, bf16[768,1536]{1,0:T(8,128)(2,1)}, u32[]{:S(2)}, u32[]{:S(2)}) %collective-permute-start.5) | collective-permute-done | bytes 2359328 | tf_op jit(solution)/shard_map/feed_scatter/ppermute | solution.py:43
  68.3 3.0 add_convert_fusion
  74.9 13.5 %collective-permute-done.6 = bf16[384,1536]{1,0:T(8,128)(2,1)} collective-permute-done((bf16[384,1536]{1,0:T(8,128)(2,1)S(1)}, bf16[384,1536]{1,0:T(8,128)(2,1)}, u32[]{:S(2)}, u32[]{:S(2)}) %collective-permute-start.6) | collective-permute-done | bytes 1179680 | tf_op jit(solution)/shard_map/feed_scatter/ppermute | solution.py:43
  88.4 1.9 add_convert_fusion.1
  90.3 2.9 collective-permute-start.7
  95.9 4.6 %collective-permute-done.7 = bf16[192,1536]{1,0:T(8,128)(2,1)S(1)} collective-permute-done((bf16[192,1536]{1,0:T(8,128)(2,1)S(1)}, bf16[192,1536]{1,0:T(8,128)(2,1)S(1)}, u32[]{:S(2)}, u32[]{:S(2)}) %collective-permute-start.7) | collective-permute-done | bytes 589856 | tf_op jit(solution)/shard_map/feed_scatter/ppermute | solution.py:43
  100.7 10.8 %collective-permute-start.8 = (bf16[96,1536]{1,0:T(8,128)(2,1)S(1)}, bf16[96,1536]{1,0:T(8,128)(2,1)S(1)}, u32[]{:S(2)}, u32[]{:S(2)}) collective-permute-start(bf16[96,1536]{1,0:T(8,128)(2,1)S(1)} %constant_dynamic-slice_fusion.2), channel_id=1, source_target_pairs={{0,96},{1,97},{2,98},{3,99},{4,100},{5,101},{6,102},{7,103},{8,40}... | collective-permute-start | bytes 884744 | tf_op jit(solution)/shard_map/feed_scatter/ppermute | solution.py:43
  113.0 2.9 collective-permute-done.8
  118.2 3.1 collective-permute-done.9
  122.2 37.6 %head.1 = (bf16[16,256,256]{2,1,0:T(8,128)(2,1)}, bf16[272,768]{1,0:T(8,128)(2,1)}) custom-call(s32[16]{0:T(128)} %get-tuple-element.75.logical, s32[16]{0:T(128)} %get-tuple-element.76.place_block, s32[1]{0:T(128)} %bitcast.4.live, bf16[4096,1536]{1,0:T(8,128)(2,1)} %all-gather.4.cloned.1.call-done.rows_ref, f32[16,2048]{1,0:T(8,128)} %constant.135.clone.table_ref, ...), custom_call_target="tpu_custom_call" | custom-call | flops 40000000000 | bytes 16000000 | tf_op jit(solution)/shard_map/head/pallas_call | solution.py:263
  159.9 2.4 collective-permute-start.2
  163.8 4.4 %collective-permute-done.2 = bf16[272,768]{1,0:T(8,128)(2,1)S(1)} collective-permute-done((bf16[272,768]{1,0:T(8,128)(2,1)}, bf16[272,768]{1,0:T(8,128)(2,1)S(1)}, u32[]{:S(2)}, u32[]{:S(2)}) %collective-permute-start.2) | collective-permute-done | bytes 417824 | tf_op jit(solution)/shard_map/head_sum/ppermute | solution.py:43
  169.9 6.4 %collective-permute-done.3 = bf16[272,768]{1,0:T(8,128)(2,1)S(1)} collective-permute-done((bf16[272,768]{1,0:T(8,128)(2,1)S(1)}, bf16[272,768]{1,0:T(8,128)(2,1)S(1)}, u32[]{:S(2)}, u32[]{:S(2)}) %collective-permute-start.3) | collective-permute-done | bytes 417824 | tf_op jit(solution)/shard_map/head_sum/ppermute | solution.py:43
  180.3 6.4 %collective-permute-done.4 = bf16[272,768]{1,0:T(8,128)(2,1)S(1)} collective-permute-done((bf16[272,768]{1,0:T(8,128)(2,1)S(1)}, bf16[272,768]{1,0:T(8,128)(2,1)S(1)}, u32[]{:S(2)}, u32[]{:S(2)}) %collective-permute-start.4) | collective-permute-done | bytes 417824 | tf_op jit(solution)/shard_map/head_sum/ppermute | solution.py:43
  189.6 11.0 %collective-permute-done.14 = bf16[192,1536]{1,0:T(8,128)(2,1)S(1)} collective-permute-done((bf16[192,1536]{1,0:T(8,128)(2,1)}, bf16[192,1536]{1,0:T(8,128)(2,1)S(1)}, u32[]{:S(2)}, u32[]{:S(2)}) %collective-permute-start.14) | collective-permute-done | bytes 589856 | tf_op jit(solution)/shard_map/feed_gather/ppermute | solution.py:43
  201.8 14.6 %collective-permute-done.15 = bf16[384,1536]{1,0:T(8,128)(2,1)S(1)} collective-permute-done((bf16[384,1536]{1,0:T(8,128)(2,1)S(1)}, bf16[384,1536]{1,0:T(8,128)(2,1)S(1)}, u32[]{:S(2)}, u32[]{:S(2)}) %collective-permute-start.15) | collective-permute-done | bytes 1179680 | tf_op jit(solution)/shard_map/feed_gather/ppermute | solution.py:43
  216.6 2.2 collective-permute-start.16
  218.8 37.9 %collective-permute-done.16 = bf16[768,1536]{1,0:T(8,128)(2,1)S(1)} collective-permute-done((bf16[768,1536]{1,0:T(8,128)(2,1)S(1)}, bf16[768,1536]{1,0:T(8,128)(2,1)S(1)}, u32[]{:S(2)}, u32[]{:S(2)}) %collective-permute-start.16) | collective-permute-done | bytes 2359328 | tf_op jit(solution)/shard_map/feed_gather/ppermute | solution.py:43
  256.7 2.3 pad_maximum_fusion.mine_ref
  259.0 15.6 %collective-permute-start.17 = (bf16[1536,1536]{1,0:T(8,128)(2,1)}, bf16[1536,1536]{1,0:T(8,128)(2,1)}, u32[]{:S(2)}, u32[]{:S(2)}) collective-permute-start(bf16[1536,1536]{1,0:T(8,128)(2,1)} %pad_maximum_fusion.mine_ref), channel_id=1, source_target_pairs={{0,8},{1,9},{2,10},{3,11},{4,12},{5,13},{6,14},{7,15},{8,0},{9,1},... | collective-permute-start | bytes 14155784 | tf_op jit(solution)/shard_map/feed_gather/ppermute | solution.py:43
  274.6 16.2 %all-to-all-start = ((bf16[16,256,256]{2,1,0:T(8,128)(2,1)}), bf16[16,256,256]{2,1,0:T(8,128)(2,1)}, u32[]{:S(2)}, u32[]{:S(2)}) async-start(bf16[16,256,256]{2,1,0:T(8,128)(2,1)} %get-tuple-element.18), calls=%async_computation | async-start | bytes 4194304 | tf_op jit(solution)/shard_map/heads_back/all_to_all | solution.py:489
  291.0 12.8 %feed_gather.1 = (f32[3072,768]{1,0:T(8,128)}, f32[768,3072]{1,0:T(8,128)}) custom-call(s32[3]{0:T(128)S(1)} %pad_add_fusion.own_chunk, bf16[1536,1536]{1,0:T(8,128)(2,1)} %pad_maximum_fusion.mine_ref, bf16[1536,1536]{1,0:T(8,128)(2,1)} %collective-permute-done.17.theirs_ref), custom_call_target="tpu_custom_call" | custom-call | bytes 28000000 | tf_op jit(solution)/shard_map/feed_gather/pallas_call | solution.py:330
  303.7 15.8 %all-to-all-done = bf16[16,256,256]{2,1,0:T(8,128)(2,1)} async-done(((bf16[16,256,256]{2,1,0:T(8,128)(2,1)}), bf16[16,256,256]{2,1,0:T(8,128)(2,1)}, u32[]{:S(2)}, u32[]{:S(2)}) %all-to-all-start) | async-done | bytes 2097184 | tf_op jit(solution)/shard_map/heads_back/all_to_all | solution.py:489
  328.5 2.7 slice.97
  332.9 3.7 %slice.98 = f32[12,192,768]{2,1,0:T(8,128)} slice(bf16[12,272,768]{2,1,0:T(8,128)(2,1)S(1)} %bitcast.98), slice={[0:12], [0:192], [0:768]} | slice | bytes 14155776 | tf_op jit(solution)/shard_map/head_place/slice | solution.py:512
  338.7 6.6 %copy.58 = f32[768,3,12,64]{0,3,2,1:T(8,128)} copy(f32[768,3,12,64]{0,3,1,2:T(8,128)} %bitcast.99) | data formatting | bytes 14155776 | tf_op jit(solution)/shard_map/head_place/transpose | solution.py:512
  345.3 8.0 %copy.62 = f32[768,2304]{1,0:T(8,128)} copy(f32[768,2304]{0,1:T(8,128)} %bitcast.100) | data formatting | bytes 14155776
  (178 shorter events, 56.5 us)
Async XLA Ops:
  7.2 86.1 %copy-start = (bf16[768,768]{1,0:T(8,128)(2,1)S(1)}, bf16[768,768]{1,0:T(8,128)(2,1)}, u32[]{:S(2)}) copy-start(bf16[768,768]{1,0:T(8,128)(2,1)} %param.24) | copy-start | bytes 3538948
  7.2 9.0 %copy-start.3 = (bf16[1,256,768]{2,1,0:T(8,128)(2,1)S(1)}, bf16[1,256,768]{2,1,0:T(8,128)(2,1)}, u32[]{:S(2)}) copy-start(bf16[1,256,768]{2,1,0:T(8,128)(2,1)} %param.32) | copy-start | bytes 1179652
  7.2 7.0 %copy-start.22 = (bf16[3072]{0:T(1024)(128)(2,1)S(1)}, bf16[3072]{0:T(1024)(128)(2,1)}, u32[]{:S(2)}) copy-start(bf16[3072]{0:T(1024)(128)(2,1)} %param.29) | copy-start | bytes 18436
  7.2 114.3 %all-gather.4.cloned.1.call-start = ((), (), s32[]{:S(2)}) async-start(), calls=%async_computation.1 | async-start | bytes 13369344 | tf_op jit(solution)/shard_map/gather_rows/all_gather | solution.py:406
  13.4 2.8 collective-permute-start
  26.6 2.4 collective-permute-start.1
  32.4 293.9 %all-gather.6.cloned.1.call-start = ((), (), s32[]{:S(2)}) async-start(), calls=%async_computation.2 | async-start | bytes 7102464 | tf_op jit(solution)/shard_map/head_sum/all_gather | solution.py:486
  39.1 29.2 %collective-permute-start.5 = (bf16[768,1536]{1,0:T(8,128)(2,1)}, bf16[768,1536]{1,0:T(8,128)(2,1)}, u32[]{:S(2)}, u32[]{:S(2)}) collective-permute-start(bf16[768,1536]{1,0:T(8,128)(2,1)} %fusion.5), channel_id=1, source_target_pairs={{0,2},{1,3},{2,0},{3,1},{4,6},{5,7},{6,4},{7,5},{8,14},{9,15},{10,... | collective-permute-start | bytes 7077896 | tf_op jit(solution)/shard_map/feed_scatter/ppermute | solution.py:43
  72.8 15.5 %collective-permute-start.6 = (bf16[384,1536]{1,0:T(8,128)(2,1)S(1)}, bf16[384,1536]{1,0:T(8,128)(2,1)}, u32[]{:S(2)}, u32[]{:S(2)}) collective-permute-start(bf16[384,1536]{1,0:T(8,128)(2,1)S(1)} %constant_dynamic-slice_fusion.4), channel_id=1, source_target_pairs={{0,6},{1,7},{2,4},{3,5},{4,2},{5,3},{6,0},{7,1},{8,10},{9,11},{10,... | collective-permute-start | bytes 3538952 | tf_op jit(solution)/shard_map/feed_scatter/ppermute | solution.py:43
  90.3 10.2 %collective-permute-start.7 = (bf16[192,1536]{1,0:T(8,128)(2,1)S(1)}, bf16[192,1536]{1,0:T(8,128)(2,1)S(1)}, u32[]{:S(2)}, u32[]{:S(2)}) collective-permute-start(bf16[192,1536]{1,0:T(8,128)(2,1)S(1)} %constant_dynamic-slice_fusion.3), channel_id=1, source_target_pairs={{0,32},{1,33},{2,34},{3,35},{4,36},{5,37},{6,38},{7,39},{8,104},{9... | collective-permute-start | bytes 1769480 | tf_op jit(solution)/shard_map/feed_scatter/ppermute | solution.py:43
  95.9 21.6 %copy-start.15 = (f32[1536]{0:T(1024)S(1)}, f32[1536]{0:T(1024)}, u32[]{:S(2)}) copy-start(f32[1536]{0:T(1024)} %get-tuple-element.94) | copy-start | bytes 18436
  95.9 21.7 %copy-start.11 = (f32[768]{0:T(1024)S(1)}, f32[768]{0:T(1024)}, u32[]{:S(2)}) copy-start(f32[768]{0:T(1024)} %get-tuple-element.65) | copy-start | bytes 9220
  100.7 15.2 %collective-permute-start.8 = (bf16[96,1536]{1,0:T(8,128)(2,1)S(1)}, bf16[96,1536]{1,0:T(8,128)(2,1)S(1)}, u32[]{:S(2)}, u32[]{:S(2)}) collective-permute-start(bf16[96,1536]{1,0:T(8,128)(2,1)S(1)} %constant_dynamic-slice_fusion.2), channel_id=1, source_target_pairs={{0,96},{1,97},{2,98},{3,99},{4,100},{5,101},{6,102},{7,103},{8,40}... | collective-permute-start | bytes 884744 | tf_op jit(solution)/shard_map/feed_scatter/ppermute | solution.py:43
  116.0 5.3 %collective-permute-start.9 = (bf16[48,1536]{1,0:T(8,128)(2,1)S(1)}, bf16[48,1536]{1,0:T(8,128)(2,1)S(1)}, u32[]{:S(2)}, u32[]{:S(2)}) collective-permute-start(bf16[48,1536]{1,0:T(8,128)(2,1)S(1)} %constant_dynamic-slice_fusion.1), channel_id=1, source_target_pairs={{0,16},{1,17},{2,18},{3,19},{4,20},{5,21},{6,22},{7,23},{8,25},{9,... | collective-permute-start | bytes 442376 | tf_op jit(solution)/shard_map/feed_scatter/ppermute | solution.py:43
  121.4 40.9 %collective-permute-start.10 = (bf16[24,1536]{1,0:T(8,128)(2,1)S(1)}, bf16[24,1536]{1,0:T(8,128)(2,1)S(1)}, u32[]{:S(2)}, u32[]{:S(2)}) collective-permute-start(bf16[24,1536]{1,0:T(8,128)(2,1)S(1)} %constant_dynamic-slice_fusion), channel_id=1, source_target_pairs={{0,17},{1,16},{2,19},{3,18},{4,21},{5,20},{6,23},{7,22},{8,24},{9,... | collective-permute-start | bytes 221192 | tf_op jit(solution)/shard_map/feed_scatter/ppermute | solution.py:43
  159.9 8.3 %collective-permute-start.2 = (bf16[272,768]{1,0:T(8,128)(2,1)}, bf16[272,768]{1,0:T(8,128)(2,1)S(1)}, u32[]{:S(2)}, u32[]{:S(2)}) collective-permute-start(bf16[272,768]{1,0:T(8,128)(2,1)} %get-tuple-element.19), channel_id=1, source_target_pairs={{0,2},{1,3},{2,0},{3,1},{4,6},{5,7},{6,4},{7,5},{8,14},{9,15},{10,... | collective-permute-start | bytes 1253384 | tf_op jit(solution)/shard_map/head_sum/ppermute | solution.py:43
  162.3 7.4 %collective-permute-start.11 = (bf16[24,1536]{1,0:T(8,128)(2,1)S(1)}, bf16[24,1536]{1,0:T(8,128)(2,1)S(1)}, u32[]{:S(2)}, u32[]{:S(2)}) collective-permute-start(bf16[24,1536]{1,0:T(8,128)(2,1)S(1)} %add_convert_fusion.8), channel_id=1, source_target_pairs={{0,17},{1,16},{2,19},{3,18},{4,21},{5,20},{6,23},{7,22},{8,24},{9,... | collective-permute-start | bytes 221192 | tf_op jit(solution)/shard_map/feed_gather/ppermute | solution.py:43
  169.3 7.0 %collective-permute-start.3 = (bf16[272,768]{1,0:T(8,128)(2,1)S(1)}, bf16[272,768]{1,0:T(8,128)(2,1)S(1)}, u32[]{:S(2)}, u32[]{:S(2)}) collective-permute-start(bf16[272,768]{1,0:T(8,128)(2,1)S(1)} %add_convert_fusion.5), channel_id=1, source_target_pairs={{0,6},{1,7},{2,4},{3,5},{4,2},{5,3},{6,0},{7,1},{8,10},{9,11},{10,... | collective-permute-start | bytes 1253384 | tf_op jit(solution)/shard_map/head_sum/ppermute | solution.py:43
  169.7 8.0 %collective-permute-start.12 = (bf16[48,1536]{1,0:T(8,128)(2,1)S(1)}, bf16[48,1536]{1,0:T(8,128)(2,1)S(1)}, u32[]{:S(2)}, u32[]{:S(2)}) collective-permute-start(bf16[48,1536]{1,0:T(8,128)(2,1)S(1)} %pad_maximum_fusion.9), channel_id=1, source_target_pairs={{0,16},{1,17},{2,18},{3,19},{4,20},{5,21},{6,22},{7,23},{8,25},{9,... | collective-permute-start | bytes 442376 | tf_op jit(solution)/shard_map/feed_gather/ppermute | solution.py:43
  176.4 10.4 %collective-permute-start.4 = (bf16[272,768]{1,0:T(8,128)(2,1)S(1)}, bf16[272,768]{1,0:T(8,128)(2,1)S(1)}, u32[]{:S(2)}, u32[]{:S(2)}) collective-permute-start(bf16[272,768]{1,0:T(8,128)(2,1)S(1)} %add_convert_fusion.4), channel_id=1, source_target_pairs={{0,1},{1,0},{2,3},{3,2},{4,5},{5,4},{6,7},{7,6},{8,9},{9,8},{10,11... | collective-permute-start | bytes 1253384 | tf_op jit(solution)/shard_map/head_sum/ppermute | solution.py:43
  178.5 9.1 %collective-permute-start.13 = (bf16[96,1536]{1,0:T(8,128)(2,1)}, bf16[96,1536]{1,0:T(8,128)(2,1)}, u32[]{:S(2)}, u32[]{:S(2)}) collective-permute-start(bf16[96,1536]{1,0:T(8,128)(2,1)} %pad_maximum_fusion.8), channel_id=1, source_target_pairs={{0,96},{1,97},{2,98},{3,99},{4,100},{5,101},{6,102},{7,103},{8,40}... | collective-permute-start | bytes 884744 | tf_op jit(solution)/shard_map/feed_gather/ppermute | solution.py:43
  189.6 11.0 %collective-permute-start.14 = (bf16[192,1536]{1,0:T(8,128)(2,1)}, bf16[192,1536]{1,0:T(8,128)(2,1)S(1)}, u32[]{:S(2)}, u32[]{:S(2)}) collective-permute-start(bf16[192,1536]{1,0:T(8,128)(2,1)} %pad_maximum_fusion.7), channel_id=1, source_target_pairs={{0,32},{1,33},{2,34},{3,35},{4,36},{5,37},{6,38},{7,39},{8,104},{9... | collective-permute-start | bytes 1769480 | tf_op jit(solution)/shard_map/feed_gather/ppermute | solution.py:43
  200.9 15.5 %collective-permute-start.15 = (bf16[384,1536]{1,0:T(8,128)(2,1)S(1)}, bf16[384,1536]{1,0:T(8,128)(2,1)S(1)}, u32[]{:S(2)}, u32[]{:S(2)}) collective-permute-start(bf16[384,1536]{1,0:T(8,128)(2,1)S(1)} %pad_maximum_fusion.4), channel_id=1, source_target_pairs={{0,6},{1,7},{2,4},{3,5},{4,2},{5,3},{6,0},{7,1},{8,10},{9,11},{10,... | collective-permute-start | bytes 3538952 | tf_op jit(solution)/shard_map/feed_gather/ppermute | solution.py:43
  216.6 40.1 %collective-permute-start.16 = (bf16[768,1536]{1,0:T(8,128)(2,1)S(1)}, bf16[768,1536]{1,0:T(8,128)(2,1)S(1)}, u32[]{:S(2)}, u32[]{:S(2)}) collective-permute-start(bf16[768,1536]{1,0:T(8,128)(2,1)S(1)} %pad_maximum_fusion.1), channel_id=1, source_target_pairs={{0,2},{1,3},{2,0},{3,1},{4,6},{5,7},{6,4},{7,5},{8,14},{9,15},{10,... | collective-permute-start | bytes 7077896 | tf_op jit(solution)/shard_map/feed_gather/ppermute | solution.py:43
  259.0 31.8 %copy-start.23 = (bf16[768]{0:T(1024)(128)(2,1)S(1)}, bf16[768]{0:T(1024)(128)(2,1)}, u32[]{:S(2)}) copy-start(bf16[768]{0:T(1024)(128)(2,1)} %param.25) | copy-start | bytes 4612
  259.0 31.8 %copy-start.24 = (bf16[768]{0:T(1024)(128)(2,1)S(1)}, bf16[768]{0:T(1024)(128)(2,1)}, u32[]{:S(2)}) copy-start(bf16[768]{0:T(1024)(128)(2,1)} %param.31) | copy-start | bytes 4612
  259.0 31.9 %copy-start.20 = (f32[256]{0:T(256)S(1)}, f32[256]{0:T(256)}, u32[]{:S(2)}) copy-start(f32[256]{0:T(256)} %get-tuple-element.64) | copy-start | bytes 3076
  259.0 31.9 %copy-start.21 = (f32[256]{0:T(256)S(1)}, f32[256]{0:T(256)}, u32[]{:S(2)}) copy-start(f32[256]{0:T(256)} %get-tuple-element.66) | copy-start | bytes 3076
  259.0 32.0 %collective-permute-start.17 = (bf16[1536,1536]{1,0:T(8,128)(2,1)}, bf16[1536,1536]{1,0:T(8,128)(2,1)}, u32[]{:S(2)}, u32[]{:S(2)}) collective-permute-start(bf16[1536,1536]{1,0:T(8,128)(2,1)} %pad_maximum_fusion.mine_ref), channel_id=1, source_target_pairs={{0,8},{1,9},{2,10},{3,11},{4,12},{5,13},{6,14},{7,15},{8,0},{9,1},... | collective-permute-start | bytes 14155784 | tf_op jit(solution)/shard_map/feed_gather/ppermute | solution.py:43
  274.6 44.9 %all-to-all-start = ((bf16[16,256,256]{2,1,0:T(8,128)(2,1)}), bf16[16,256,256]{2,1,0:T(8,128)(2,1)}, u32[]{:S(2)}, u32[]{:S(2)}) async-start(bf16[16,256,256]{2,1,0:T(8,128)(2,1)} %get-tuple-element.18), calls=%async_computation | async-start | bytes 4194304 | tf_op jit(solution)/shard_map/heads_back/all_to_all | solution.py:489
  303.7 18.5 %copy-start.13 = (f32[768]{0:T(1024)S(1)}, f32[768]{0:T(1024)}, u32[]{:S(2)}) copy-start(f32[768]{0:T(1024)} %copy-done.12) | copy-start | bytes 9220
  337.2 16.1 %copy-start.14 = (f32[768]{0:T(1024)}, f32[768]{0:T(1024)S(1)}, u32[]{:S(2)}) copy-start(f32[768]{0:T(1024)S(1)} %get-tuple-element.128) | copy-start | bytes 9220
  (20 other events, 41.2 us)
Sparse Core Ops, SparseCore 0:
  32.5 77.2 all-gather.3
  187.7 55.5 all-gather.5

commit v2 on v1

v2 whole, which is shorter than its diff:
```python
import math

import jax
import jax.numpy as jnp
import numpy as np
from jax import lax
from jax.experimental import pallas as pl
from jax.experimental.pallas import tpu as pltpu
from jax.sharding import PartitionSpec as P

H = 12
DH = 64
D = 768
FF = 3072
ROT = 16
TOK = 256
SEQ_DEV = 16
LONG_BLOCKS = 8
EPS = 1e-05
F32 = jnp.float32
BF16 = jnp.bfloat16
TILE = 512
PROJECT = 4
COLLECT = 4
AHEAD = 8
FEED_CUT = 384
HEAD_ROWS = 272


AXES = ("y", "zl", "c", "x", "zh")
SIZES = (4, 2, 2, 4, 2)
SEQ = ("y", "zl", "c")


def place(index):
    at = {}
    for name, size in zip(reversed(AXES), reversed(SIZES)):
        index, at[name] = divmod(index, size)
    return at


def index_of(at):
    index = 0
    for name, size in zip(AXES, SIZES):
        index = index * size + at[name]
    return index


def swap(value, partner):
    pairs = [(i, index_of(partner(place(i)))) for i in range(math.prod(SIZES))]
    return lax.ppermute(value, AXES, pairs)


def here():
    return {name: lax.axis_index(name) for name in AXES}


def other(axis):
    return lambda at: {**at, axis: 1 - at[axis]}


def ring_next(i, core, step):
    near, far = i ^ 1, 3 - i
    if isinstance(core, int):
        return near if step == core else far
    return jnp.where(core == step, near, far)


def ring_partner(axis, step):
    return lambda at: {**at, axis: ring_next(at[axis], at["c"], step)}


def ring_bits(i, core):
    inner = ((i == 1) | (i == 2)).astype(jnp.int32)
    upper = (i >= 2).astype(jnp.int32)
    return jnp.where(core == 0, inner, upper), jnp.where(core == 0, upper, inner)


def ring_chunk(i, core):
    first, second = ring_bits(i, core)
    return first * 2 + second


def ring_slots(i, core):
    one, two = ring_next(i, core, 1), ring_next(i, core, 0)
    return [i, one, two, ring_next(two, core, 1)]


def added(*values):
    total = values[0].astype(F32)
    for value in values[1:]:
        total = total + value.astype(F32)
    return total.astype(BF16)


def half(value, which):
    rows = value.shape[1] // 2
    return lax.dynamic_slice_in_dim(value, which * rows, rows, 1)


def after(value, *earlier):
    return lax.optimization_barrier((value, *earlier))[0]


def norm_kernel(
    x_ref, grad_ref, gain1_ref, shift1_ref, gain2_ref, shift2_ref,
    rows_ref, own_ref, normal_ref, rate_ref,
):
    def row(ref):
        return ref[...].astype(F32).reshape(1, D)

    values = x_ref[...].astype(F32)
    centre = values - jnp.mean(values, axis=-1, keepdims=True)
    spread = jnp.mean(centre * centre, axis=-1, keepdims=True)
    rate = lax.rsqrt(spread + EPS)
    normal = centre * rate
    rows_ref[:, :D] = (normal * row(gain1_ref) + row(shift1_ref)).astype(BF16)
    own_ref[:, :D] = (normal * row(gain2_ref) + row(shift2_ref)).astype(BF16)
    rows_ref[:, D:] = grad_ref[...]
    own_ref[:, D:] = grad_ref[...]
    normal_ref[...] = normal
    rate_ref[...] = jnp.broadcast_to(rate, (TOK, 128))


def norms(x, grad_rows, gains):
    return pl.pallas_call(
        norm_kernel,
        out_shape=(
            jax.ShapeDtypeStruct((TOK, 2 * D), BF16),
            jax.ShapeDtypeStruct((TOK, 2 * D), BF16),
            jax.ShapeDtypeStruct((TOK, D), F32),
            jax.ShapeDtypeStruct((TOK, 128), F32),
        ),
        cost_estimate=pl.CostEstimate(
            flops=3 * 10**8, bytes_accessed=5 * 10**6, transcendentals=256
        ),
    )(x, grad_rows, *gains)


def contract(left, right, dims):
    return lax.dot_general(left, right, (dims, ((), ())), preferred_element_type=F32)


def rotate_rows(rows, cosine, sine):
    first, second = rows[0:8], rows[8:16]
    return jnp.concatenate(
        [first * cosine - second * sine, second * cosine + first * sine, rows[16:]], 0
    )


def head_kernel(
    ids, places, which,
    rows_hbm, table_ref, wo_ref, wq_ref, wk_ref, wv_ref, bq_ref, bk_ref, bv_ref, norm_ref, extra_ref,
    send_hbm, grad_ref,
    rows_ref, in_sem, out_sem, w_ref, bias_ref, t_ref, q_ref, k_ref, v_ref, g_ref, s_ref, p_ref, dk_ref, dv_ref, o_ref, gw_ref, go_ref, gb_ref, gc_ref,
):
    def place_block(b):
        return lax.div(places[b * TOK], TOK)

    def logical(b):
        ident = ids[b * TOK]
        return place_block(b) + jnp.where(ident == 0, 0, LONG_BLOCKS + 2 * (ident - 1))

    def fetch(b):
        at = pl.multiple_of(b * TOK, TOK)
        return pltpu.make_async_copy(
            rows_hbm.at[pl.ds(at, TOK)], rows_ref.at[pl.ds(at, TOK)], in_sem.at[b]
        )

    def post(b):
        frm = pl.multiple_of(logical(b) * TOK, TOK)
        return pltpu.make_async_copy(
            o_ref.at[:, pl.ds(frm, TOK)], send_hbm.at[b], out_sem.at[b]
        )

    for b in range(AHEAD):
        fetch(b).start()
    odd = which[0] % 2 == 1
    for n, (w, bias) in enumerate(((wq_ref, bq_ref), (wk_ref, bk_ref), (wv_ref, bv_ref))):
        block = jnp.where(odd, w[:, DH:].astype(F32), w[:, :DH].astype(F32))
        w_ref[n * DH : n * DH + DH, :] = block.T.astype(BF16)
        row = jnp.where(odd, bias[:, DH:], bias[:, :DH])
        bias_ref[n * DH : n * DH + DH, :] = jnp.broadcast_to(row, (128, DH)).T

    def project(step, _):
        for n in range(PROJECT):
            fetch(step * PROJECT + n).wait()

        for n in range(PROJECT):
            ahead = step * PROJECT + n + AHEAD

            @pl.when(ahead < SEQ_DEV)
            def _():
                fetch(ahead).start()

        at = pl.multiple_of(step * PROJECT * TOK, TOK)
        rows = rows_ref[pl.ds(at, PROJECT * TOK), :]
        mixed_all = contract(w_ref[...], rows[:, :D], ((1,), (1,))) + bias_ref[:, 0:1]
        grad_all = contract(wo_ref[...], rows[:, D:], ((1,), (1,)))
        for n in range(PROJECT):
            b = step * PROJECT + n
            to = pl.multiple_of(logical(b) * TOK, TOK)
            pos = pl.multiple_of(place_block(b) * TOK, TOK)
            cosine = table_ref[0:8, pl.ds(pos, TOK)]
            sine = table_ref[8:16, pl.ds(pos, TOK)]
            mixed = mixed_all[:, n * TOK : n * TOK + TOK]
            query = rotate_rows(mixed[0:64], cosine, sine) * 0.125
            key = rotate_rows(mixed[64:128], cosine, sine)
            parts = (query, key, mixed[128:192], grad_all[:, n * TOK : n * TOK + TOK])
            for m, (part, ref) in enumerate(zip(parts, (q_ref, k_ref, v_ref, g_ref))):
                part = part.astype(BF16)
                t_ref[m * 64 : m * 64 + 64, pl.ds(to, TOK)] = part
                ref[pl.ds(to, TOK), :] = part.T
        return 0

    lax.fori_loop(0, SEQ_DEV // PROJECT, project, 0)

    def attend(task):
        base = task * TILE
        full = task if task < 4 else 0
        last = full * TILE
        small = TILE // 2
        corner = (
            (base, last, 0, True),
            (base + small, last + small, small, True),
        )

        def keys_of(part):
            return pl.ds(part[0], small if part[3] else TILE)

        def slot_of(part):
            return pl.ds(part[1], small if part[3] else TILE)

        def lanes(part):
            return slice(part[2], TILE)

        def widen(part, value, fill):
            if part[2] == 0:
                return value
            return jnp.concatenate([jnp.full(value.shape, fill, F32), value], 1)

        q_t = t_ref[0:64, pl.ds(base, TILE)]
        g_t = t_ref[192:256, pl.ds(base, TILE)]

        def score(part, top):
            scores = contract(k_ref[keys_of(part), :], q_t[:, lanes(part)], ((1,), (0,)))
            if part[3]:
                key_at = lax.broadcasted_iota(jnp.int32, scores.shape, 0)
                query_at = lax.broadcasted_iota(jnp.int32, scores.shape, 1)
                scores = jnp.where(key_at <= query_at, scores, -1e30)
            s_ref[slot_of(part), lanes(part)] = scores
            return jnp.maximum(top, widen(part, jnp.max(scores, axis=0, keepdims=True), -1e30))

        def weigh(part, carry):
            total, dot_total, out = carry
            raised = jnp.exp(s_ref[slot_of(part), lanes(part)] - top[:, lanes(part)])
            s_ref[slot_of(part), lanes(part)] = raised
            grads = contract(v_ref[keys_of(part), :], g_t[:, lanes(part)], ((1,), (0,)))
            p_ref[slot_of(part), lanes(part)] = grads
            total = total + widen(part, jnp.sum(raised, axis=0, keepdims=True), 0.0)
            dot_total = dot_total + widen(
                part, jnp.sum(raised * grads, axis=0, keepdims=True), 0.0
            )
            out = out + widen(
                part,
                contract(t_ref[128:192, keys_of(part)], raised.astype(BF16), ((1,), (0,))),
                0.0,
            )
            return total, dot_total, out

        def back(part, grad_q):
            probs = s_ref[slot_of(part), lanes(part)] * scale[:, lanes(part)]
            grads = probs * (p_ref[slot_of(part), lanes(part)] - row_total[:, lanes(part)])
            grads = grads.astype(BF16)
            queries = pl.ds(base + part[2], TILE - part[2])
            grad_v = contract(probs.astype(BF16), g_ref[queries, :], ((1,), (0,)))
            grad_k = contract(grads, q_ref[queries, :], ((1,), (0,)))
            if part[3]:
                dv_ref[keys_of(part), :] = grad_v
                dk_ref[keys_of(part), :] = grad_k
            else:
                dv_ref[keys_of(part), :] += grad_v
                dk_ref[keys_of(part), :] += grad_k
            return grad_q + widen(
                part, contract(t_ref[64:128, keys_of(part)], grads, ((1,), (0,))), 0.0
            )

        def every(step, carry):
            for part in (*corner, *[(j * TILE, j * TILE, 0, False) for j in range(full)]):
                carry = step(part, carry)
            return carry

        top = every(score, jnp.full((1, TILE), -1e30, F32))
        zero = jnp.zeros((1, TILE), F32)
        total, dot_total, out = every(weigh, (zero, zero, jnp.zeros((64, TILE), F32)))
        scale = 1.0 / total
        row_total = dot_total * scale
        o_ref[0:64, pl.ds(base, TILE)] = (out * scale).astype(BF16)
        grad_q = every(back, jnp.zeros((64, TILE), F32)) * 0.125
        cosine = table_ref[0:8, pl.ds(last, TILE)]
        sine = table_ref[8:16, pl.ds(last, TILE)]
        o_ref[64:128, pl.ds(base, TILE)] = rotate_rows(grad_q, cosine, -sine).astype(BF16)

    for task in range(8):
        attend(task)

    def turn_back(task):
        base = task * TILE
        pos = base if task < 4 else 0
        cosine = table_ref[0:8, pl.ds(pos, TILE)]
        sine = table_ref[8:16, pl.ds(pos, TILE)]
        grad_k = dk_ref[pl.ds(base, TILE), :].T
        o_ref[128:192, pl.ds(base, TILE)] = rotate_rows(grad_k, cosine, -sine).astype(BF16)
        o_ref[192:256, pl.ds(base, TILE)] = dv_ref[pl.ds(base, TILE), :].T.astype(BF16)

    for task in range(8):
        turn_back(task)
    gw_ref[...] = jnp.zeros_like(gw_ref)
    go_ref[...] = jnp.zeros_like(go_ref)
    gb_ref[...] = jnp.zeros_like(gb_ref)
    gc_ref[...] = jnp.zeros_like(gc_ref)

    def collect(step, _):
        blocks = []
        for n in range(COLLECT):
            b = step * COLLECT + n
            post(b).start()
            blocks.append(o_ref[:, pl.ds(pl.multiple_of(logical(b) * TOK, TOK), TOK)])
        block = jnp.concatenate(blocks, 1)
        at = pl.multiple_of(step * COLLECT * TOK, TOK)
        grads = block[64:256]
        gw_ref[...] += contract(grads, rows_ref[pl.ds(at, COLLECT * TOK), :D], ((1,), (0,)))
        go_ref[...] += contract(block[0:64], rows_ref[pl.ds(at, COLLECT * TOK), D:], ((1,), (0,)))
        gb_ref[...] += contract(jnp.ones((8, COLLECT * TOK), BF16), grads, ((1,), (1,)))
        gc_ref[...] += jnp.broadcast_to(
            jnp.sum(grads.astype(F32), axis=1, keepdims=True), (192, 128)
        )
        return 0

    lax.fori_loop(0, SEQ_DEV // COLLECT, collect, 0)
    grad_ref[0:192, :] = gw_ref[...].astype(BF16)
    alive = which[1] == 1
    weights = w_ref[...].astype(F32)
    sums = gc_ref[:, 0:1]
    shift_grad = jnp.sum(sums * weights, axis=0, keepdims=True)
    gain_grad = jnp.sum(
        weights * (gw_ref[...] - sums * norm_ref[1:2, :]), axis=0, keepdims=True
    ) / norm_ref[0:1, :]
    bias_row = jnp.concatenate([gb_ref[0:1, :], jnp.zeros((1, D - 192), F32)], 1)
    own = jnp.concatenate([gain_grad, shift_grad, bias_row, jnp.zeros((5, D), F32)], 0)
    own = jnp.where(alive, own, 0.0)
    grad_ref[192:256, :] = go_ref[...].astype(BF16)
    grad_ref[256:272, :] = jnp.concatenate([own, extra_ref[...]], 0).astype(BF16)
    for b in range(SEQ_DEV):
        post(b).wait()


def one_head(ids, places, which, rows, table, output_weight, weight, bias, norm, extra):
    count = SEQ_DEV * TOK

    def whole(*shape):
        return pl.BlockSpec(shape, lambda s, *_: (0,) * len(shape))

    def cut(rows, n):
        return pl.BlockSpec((rows, 2 * DH), lambda s, l, p, w: (0, n * (H // 2) + w[0] // 2))

    return pl.pallas_call(
        head_kernel,
        out_shape=(
            jax.ShapeDtypeStruct((SEQ_DEV, 256, TOK), BF16),
            jax.ShapeDtypeStruct((272, D), BF16),
        ),
        grid_spec=pltpu.PrefetchScalarGridSpec(
            num_scalar_prefetch=3,
            grid=(1,),
            in_specs=[
                pl.BlockSpec(memory_space=pl.ANY),
                whole(16, 2048),
                pl.BlockSpec((DH, D), lambda s, l, p, w: (w[0], 0)),
                *[cut(D, n) for n in range(3)],
                *[cut(1, n) for n in range(3)],
                whole(8, D),
                whole(8, D),
            ],
            out_specs=(pl.BlockSpec(memory_space=pl.ANY), whole(272, D)),
            scratch_shapes=[
                pltpu.VMEM((count, 2 * D), BF16),
                pltpu.SemaphoreType.DMA((SEQ_DEV,)),
                pltpu.SemaphoreType.DMA((SEQ_DEV,)),
                pltpu.VMEM((192, D), BF16),
                pltpu.VMEM((192, 128), F32),
                pltpu.VMEM((256, count), BF16),
                pltpu.VMEM((count, DH), BF16),
                pltpu.VMEM((count, DH), BF16),
                pltpu.VMEM((count, DH), BF16),
                pltpu.VMEM((count, DH), BF16),
                pltpu.VMEM((4 * TILE, TILE), F32),
                pltpu.VMEM((4 * TILE, TILE), F32),
                pltpu.VMEM((count, DH), F32),
                pltpu.VMEM((count, DH), F32),
                pltpu.VMEM((256, count), BF16),
                pltpu.VMEM((192, D), F32),
                pltpu.VMEM((DH, D), F32),
                pltpu.VMEM((8, 192), F32),
                pltpu.VMEM((192, 128), F32),
            ],
        ),
        compiler_params=pltpu.CompilerParams(vmem_limit_bytes=56 * 2**20),
        cost_estimate=pl.CostEstimate(
            flops=24 * 10**9, bytes_accessed=12 * 10**6, transcendentals=4 * 10**6
        ),
    )(ids, places, which, rows, table, output_weight, *[weight] * 3, *[bias] * 3, norm, extra)


def rotary_table():
    freq = (1.0 / 10000.0 ** (np.arange(8, dtype=np.float64) * 2.0 / ROT)).astype(np.float32)
    angle = np.arange(2048, dtype=np.float32)[None, :] * freq[:, None]
    angle = angle.astype(np.float64)
    return np.concatenate([np.cos(angle), np.sin(angle)], 0).astype(np.float32)


def gelu_and_slope(values):
    cdf = 0.5 * (1.0 + lax.erf(values * np.float32(math.sqrt(0.5))))
    pdf = jnp.exp(-0.5 * values * values) * np.float32(1.0 / math.sqrt(2.0 * math.pi))
    return values * cdf, cdf + values * pdf


def feed_kernel(
    where, own_ref, other_ref, up_ref, down_ref, bias_ref, *refs,
):
    if len(refs) == 4:
        sum_ref, bias_sum_ref, rows_ref, total_ref = refs
    else:
        before_ref, sum_ref, bias_sum_ref, mine_ref, theirs_ref, total_ref = refs
    step = pl.program_id(0)
    second = jnp.concatenate([own_ref[:, :D], other_ref[:, :D]], 0)
    grads = jnp.concatenate([own_ref[:, D:], other_ref[:, D:]], 0)
    hidden = contract(second, up_ref[...], ((1,), (0,))) + bias_ref[...]
    active, slope = gelu_and_slope(hidden)
    active = active.astype(BF16)
    grad_hidden = (contract(grads, down_ref[...], ((1,), (1,))) * slope).astype(BF16)
    sum_ref[0] = contract(active, grads, ((0,), (0,))).astype(BF16)
    sum_ref[1] = contract(grad_hidden, second, ((0,), (0,))).astype(BF16)
    bias_sum_ref[...] = jnp.sum(grad_hidden.astype(F32), axis=0, keepdims=True)
    feed_part = contract(active, down_ref[...], ((1,), (0,)))
    back_part = contract(grad_hidden, up_ref[...], ((1,), (1,)))

    @pl.when(step == 0)
    def _():
        total_ref[:, :D] = feed_part
        total_ref[:, D:] = back_part

    @pl.when(step > 0)
    def _():
        total_ref[:, :D] += feed_part
        total_ref[:, D:] += back_part

    @pl.when(step == pl.num_programs(0) - 1)
    def _():
        if len(refs) == 4:
            rows_ref[...] = total_ref[...]
        else:
            mine_ref[...] = total_ref[:TOK, :] + before_ref[:TOK, :]
            theirs_ref[...] = (total_ref[TOK:, :] + before_ref[TOK:, :]).astype(BF16)


def feed_half(where, own, got, up_weight, down_weight, up_bias, *before):
    units, cut = FF // 4, FEED_CUT
    steps = units // cut
    rows = pl.BlockSpec((TOK, 2 * D), lambda s, w: (0, 0))
    both = pl.BlockSpec((2 * TOK, 2 * D), lambda s, w: (0, 0))
    if before:
        row_shapes = (
            jax.ShapeDtypeStruct((TOK, 2 * D), F32),
            jax.ShapeDtypeStruct((TOK, 2 * D), BF16),
        )
    else:
        row_shapes = (jax.ShapeDtypeStruct((2 * TOK, 2 * D), F32),)
    return pl.pallas_call(
        feed_kernel,
        out_shape=(
            jax.ShapeDtypeStruct((2, units, D), BF16),
            jax.ShapeDtypeStruct((1, units), F32),
            *row_shapes,
        ),
        grid_spec=pltpu.PrefetchScalarGridSpec(
            num_scalar_prefetch=1,
            grid=(steps,),
            in_specs=[
                rows,
                rows,
                pl.BlockSpec((D, cut), lambda s, w: (0, w[0] * steps + s)),
                pl.BlockSpec((cut, D), lambda s, w: (w[0] * steps + s, 0)),
                pl.BlockSpec((1, cut), lambda s, w: (0, w[0] * steps + s)),
                *[both] * len(before),
            ],
            out_specs=(
                pl.BlockSpec((2, cut, D), lambda s, w: (0, s, 0)),
                pl.BlockSpec((1, cut), lambda s, w: (0, s)),
                *([rows] * 2 if before else [both]),
            ),
            scratch_shapes=[pltpu.VMEM((2 * TOK, 2 * D), F32)],
        ),
        compiler_params=pltpu.CompilerParams(vmem_limit_bytes=58 * 2**20),
        cost_estimate=pl.CostEstimate(
            flops=4 * 10**9, bytes_accessed=8 * 10**6, transcendentals=10**6
        ),
    )(where, own, got, up_weight, down_weight, up_bias, *before)


def round_call(kernel, scalars, values, shapes, later=()):
    def whole(shape):
        return pl.BlockSpec(shape, lambda s, w: (0,) * len(shape))

    return pl.pallas_call(
        kernel,
        out_shape=tuple(jax.ShapeDtypeStruct(shape, BF16) for shape in shapes),
        grid_spec=pltpu.PrefetchScalarGridSpec(
            num_scalar_prefetch=1,
            grid=(1,),
            in_specs=[
                *[whole(value.shape) for value in values],
                *[pl.BlockSpec(memory_space=pl.ANY)] * len(later),
            ],
            out_specs=tuple(whole(shape) for shape in shapes),
        ),
        compiler_params=pltpu.CompilerParams(vmem_limit_bytes=58 * 2**20),
        cost_estimate=pl.CostEstimate(flops=0, bytes_accessed=0, transcendentals=0),
    )(scalars, *values, *later)


def hold_kernel(value_ref, *refs):
    del value_ref, refs


def hold(value, *later):
    return pl.pallas_call(
        hold_kernel,
        out_shape=jax.ShapeDtypeStruct(value.shape, value.dtype),
        in_specs=[pl.BlockSpec(memory_space=pl.ANY)] * (1 + len(later)),
        out_specs=pl.BlockSpec(memory_space=pl.ANY),
        input_output_aliases={0: 0},
        cost_estimate=pl.CostEstimate(flops=0, bytes_accessed=0, transcendentals=0),
    )(value, *later)


def quad_kernel(which, own_ref, *refs):
    values = [own_ref[...].astype(F32), *[ref[...].astype(F32) for ref in refs[:3]]]
    rows = []
    for k in range(4):
        row = values[3]
        for r in range(3):
            row = jnp.where((which[0] ^ k) == r, values[r], row)
        rows.append(row)
    refs[-1][...] = jnp.concatenate(rows, 1).astype(BF16)


def line_kernel(which, own_ref, *refs):
    rows = own_ref.shape[1]
    for r, ref in enumerate((own_ref, *refs[:3])):
        to = pl.multiple_of((which[0] ^ r) * rows, rows)
        refs[-1][:, pl.ds(to, rows), :] = ref[...]


def place_feed_kernel(where, mine_ref, theirs_ref, *refs):
    down_ref, up_ref = refs[-2:]

    def put(ref):
        down_ref[...] = ref[0].astype(F32)
        up_ref[...] = ref[1].astype(F32).T

    @pl.when(pl.program_id(0) == 0)
    def _():
        put(mine_ref)

    @pl.when(pl.program_id(0) == 1)
    def _():
        put(theirs_ref)


def place_feed(where, mine, theirs, placed):
    rows = FF // 8
    block = pl.BlockSpec((2, rows, D), lambda s, w: (0, 0, 0))
    kept = [pl.BlockSpec(memory_space=pl.ANY)] * len(placed)
    return pl.pallas_call(
        place_feed_kernel,
        out_shape=(
            jax.ShapeDtypeStruct((FF, D), F32),
            jax.ShapeDtypeStruct((D, FF), F32),
        ),
        grid_spec=pltpu.PrefetchScalarGridSpec(
            num_scalar_prefetch=1,
            grid=(2,),
            in_specs=[block, block, *kept],
            out_specs=(
                pl.BlockSpec((rows, D), lambda s, w: (w[s], 0)),
                pl.BlockSpec((D, rows), lambda s, w: (0, w[s])),
            ),
        ),
        input_output_aliases={3: 0, 4: 1} if placed else {},
        cost_estimate=pl.CostEstimate(flops=0, bytes_accessed=0, transcendentals=0),
    )(where, mine, theirs, *placed)


def place_heads_kernel(
    sums_ref, rest_ref, input_ref, output_ref,
    gain1_ref, shift1_ref, bias_ref, out_bias_ref, down_bias_ref, gain2_ref, shift2_ref, up_bias_ref,
):
    rows = sums_ref[...].reshape(H * DH, D).astype(F32)

    @pl.when(pl.program_id(1) < 3)
    def _():
        input_ref[...] = rows.T

    @pl.when(pl.program_id(1) == 3)
    def _():
        output_ref[...] = rows

    @pl.when((pl.program_id(0) == 0) & (pl.program_id(1) == 0))
    def _():
        rest = rest_ref[...].astype(F32)
        total = jnp.sum(rest, axis=0)
        for ref, n in (
            (gain1_ref, 0),
            (shift1_ref, 1),
            (out_bias_ref, 8),
            (down_bias_ref, 8),
            (gain2_ref, 9),
            (shift2_ref, 10),
        ):
            ref[...] = total[n : n + 1].reshape(D)
        bias = [rest[h, 2:3, n * DH : n * DH + DH] for n in range(3) for h in range(H)]
        bias_ref[...] = jnp.concatenate(bias, 1).reshape(3 * D)
        up = [sum(rest[d, n : n + 1] for d in range(c, SEQ_DEV, 2)) for c in (0, 1) for n in (11, 12)]
        up_bias_ref[...] = jnp.concatenate(up, 1).reshape(FF)


def place_heads(sums):
    sizes = (D, D, 3 * D, D, D, D, D, FF)
    return pl.pallas_call(
        place_heads_kernel,
        out_shape=(
            jax.ShapeDtypeStruct((D, 3 * D), F32),
            jax.ShapeDtypeStruct((D, D), F32),
            *[jax.ShapeDtypeStruct((size,), F32) for size in sizes],
        ),
        grid=(1, 4),
        in_specs=[
            pl.BlockSpec((H, DH, D), lambda p, n: (0, n, 0)),
            pl.BlockSpec((SEQ_DEV, 16, D), lambda p, n: (0, 16, 0)),
        ],
        out_specs=(
            pl.BlockSpec((D, D), lambda p, n: (0, jnp.minimum(n, 2))),
            pl.BlockSpec((H * DH, D), lambda p, n: (0, 0)),
            *[pl.BlockSpec((size,), lambda p, n: (0,)) for size in sizes],
        ),
        compiler_params=pltpu.CompilerParams(vmem_limit_bytes=58 * 2**20),
        cost_estimate=pl.CostEstimate(flops=0, bytes_accessed=0, transcendentals=0),
    )(sums, sums)


def norm_back(normal, rate, grad, gain):
    scaled = grad * gain
    return rate * (
        scaled
        - jnp.mean(scaled, axis=-1, keepdims=True)
        - normal * jnp.mean(scaled * normal, axis=-1, keepdims=True)
    )


def finish_kernel(
    back_ref, x_ref, grad_ref, normal_ref, rate_ref, parts_ref, gain1_ref, gain2_ref,
    out_bias_ref, down_bias_ref, out_weight_ref, in_weight_ref,
    result_ref, grad_x_ref,
):
    def row(ref):
        return ref[...].astype(F32).reshape(1, D)

    attended = jnp.concatenate([back_ref[h, :DH] for h in range(H)], 0)
    out = contract(attended, out_weight_ref[...], ((0,), (0,)))
    out = out + parts_ref[:, :D] + row(out_bias_ref) + row(down_bias_ref)
    result_ref[...] = (x_ref[...].astype(F32) + out).astype(BF16)
    mixed = jnp.concatenate(
        [back_ref[h, n * DH : (n + 1) * DH] for n in range(1, 4) for h in range(H)], 0
    )
    grad_first = contract(mixed, in_weight_ref[...], ((0,), (1,)))
    normal, rate = normal_ref[...], rate_ref[:, 0:1]
    grad_x_ref[...] = (
        grad_ref[...].astype(F32)
        + norm_back(normal, rate, grad_first, row(gain1_ref))
        + norm_back(normal, rate, parts_ref[:, D:], row(gain2_ref))
    )


def finish(back, *values):
    def whole(value):
        return pl.BlockSpec(value.shape, lambda s: (0,) * value.ndim)

    return pl.pallas_call(
        finish_kernel,
        out_shape=(
            jax.ShapeDtypeStruct((TOK, D), BF16),
            jax.ShapeDtypeStruct((TOK, D), F32),
        ),
        grid=(1,),
        in_specs=[
            pl.BlockSpec((H, 256, TOK), lambda s: (0, 0, 0)),
            *[whole(value) for value in values],
        ],
        out_specs=(
            pl.BlockSpec((TOK, D), lambda s: (0, 0)),
            pl.BlockSpec((TOK, D), lambda s: (0, 0)),
        ),
        compiler_params=pltpu.CompilerParams(vmem_limit_bytes=58 * 2**20),
        cost_estimate=pl.CostEstimate(flops=0, bytes_accessed=0, transcendentals=0),
    )(back, *values)


def body(
    tokens,
    sequence,
    positions,
    first_gain,
    first_shift,
    input_weight,
    input_bias,
    output_weight,
    output_bias,
    second_gain,
    second_shift,
    up_weight,
    up_bias,
    down_weight,
    down_bias,
    cotangent,
):
    at = here()
    seq = at["y"] * 4 + at["zl"] * 2 + at["c"]
    core = at["c"]
    grad_rows = cotangent[0]
    grad_float = grad_rows.astype(F32)

    with jax.named_scope("norms"):
        rows, own, normal, rate = norms(
            tokens[0], grad_rows, (first_gain, first_shift, second_gain, second_shift)
        )

    with jax.named_scope("gather_rows"):
        rows_all = lax.all_gather(rows, SEQ, axis=0, tiled=True)

    with jax.named_scope("feed"):
        first_bit, second_bit = ring_bits(at["x"], core)
        got = swap(own, other("c"))
        weights = (own, got, up_weight, down_weight, up_bias.astype(F32)[None])
        sent, sent_bias, before = feed_half((core * 2 + 1 - first_bit)[None], *weights)
        kept, kept_bias, parts, theirs = feed_half(
            (core * 2 + first_bit)[None], *weights, before
        )
        parts = parts + swap(theirs, other("c")).astype(F32)
        grad_second = parts[:, D:]
        extra = jnp.concatenate(
            [
                jnp.sum(grad_float, axis=0)[None],
                jnp.sum(grad_second * normal, axis=0)[None],
                jnp.sum(grad_second, axis=0)[None],
                jnp.where(first_bit == 0, kept_bias, sent_bias),
                jnp.where(first_bit == 0, sent_bias, kept_bias),
                jnp.zeros((3, D), F32),
            ],
            0,
        )

    with jax.named_scope("feed_scatter"):
        feed_sum = added(kept, swap(sent, ring_partner("x", 0)))
        got = swap(half(feed_sum, 1 - second_bit), ring_partner("x", 1))
        feed_sum = added(half(feed_sum, second_bit), got)
        feed_sum = feed_sum.reshape(2, 16, FF // 128, D).transpose(1, 0, 2, 3)
        spread = lax.all_to_all(feed_sum, ("y", "zl", "zh"), 0, 0, tiled=True)

    with jax.named_scope("head"):
        which = jnp.stack([jnp.minimum(seq, H - 1), (seq < H).astype(jnp.int32)])
        norm = jnp.stack([first_gain, first_shift] * 4).astype(F32)
        send, head_sum = one_head(
            sequence[0],
            positions[0],
            which.astype(jnp.int32),
            rows_all,
            jnp.asarray(rotary_table()),
            output_weight,
            input_weight,
            input_bias.astype(F32)[None],
            norm,
            after(extra, feed_sum),
        )

    def scalars(*values):
        return jnp.stack(values).astype(jnp.int32)

    with jax.named_scope("rounds"):
        def flipped(*axes):
            return lambda p: {**p, **{axis: 1 - p[axis] for axis in axes}}

        def along_y(r):
            return lambda p: {**p, "y": p["y"] ^ r}

        spread = hold(spread, head_sum)
        feed_sum = added(*[spread[n] for n in range(16)])
        (feed_sum,) = round_call(
            quad_kernel,
            scalars(at["zl"] * 2 + at["zh"]),
            (feed_sum, *[swap(feed_sum, flipped(*f)) for f in (("zh",), ("zl",), ("zl", "zh"))]),
            ((2, 96, D),),
        )
        head_sum = added(head_sum, swap(head_sum, other("zh")))
        got = [swap(feed_sum, along_y(r)) for r in (1, 2, 3)]
        (feed_sum,) = round_call(
            line_kernel, scalars(at["y"]), (feed_sum, *got), ((2, FF // 8, D),)
        )
        back = lax.all_to_all(hold(send, feed_sum), SEQ, 0, 0, tiled=True)
        for step in range(2):
            head_sum = added(head_sum, swap(head_sum, ring_partner("x", step)))
        one = swap(feed_sum, ring_partner("x", 1))
        two = swap(feed_sum, ring_partner("x", 0))
        sums = lax.all_gather(hold(head_sum, back, one, two), SEQ, axis=0)

    with jax.named_scope("heads_back"):
        result, grad_tokens = finish(
            back, tokens[0], grad_rows, normal, rate, parts, first_gain, second_gain,
            output_bias, down_bias, output_weight, input_weight,
        )
        result, grad_tokens = result[None], grad_tokens[None]

    with jax.named_scope("feed_gather"):
        blocks = [
            [c * 4 + ring_chunk(x, c) for x in ring_slots(at["x"], c)] for c in (core, 1 - core)
        ]
        where = [scalars(blocks[0][n], blocks[1][n]) for n in range(4)]
        last = swap(one, ring_partner("x", 0))
        theirs = swap(feed_sum, other("c"))
        placed = place_feed(where[0], hold(feed_sum, grad_tokens), theirs, ())
        placed = place_feed(where[1], one, swap(one, other("c")), placed)
        placed = place_feed(where[2], two, swap(two, other("c")), placed)
        last = hold(last, placed[0])
        placed = place_feed(where[3], last, swap(last, other("c")), placed)
        grad_down_weight, grad_up_weight = placed

    with jax.named_scope("head_place"):
        (
            grad_input_weight,
            grad_output_weight,
            grad_first_gain,
            grad_first_shift,
            grad_input_bias,
            grad_output_bias,
            grad_down_bias,
            grad_second_gain,
            grad_second_shift,
            grad_up_bias,
        ) = place_heads(sums)
    return (
        result,
        grad_tokens,
        grad_first_gain,
        grad_first_shift,
        grad_input_weight,
        grad_input_bias,
        grad_output_weight,
        grad_output_bias,
        grad_second_gain,
        grad_second_shift,
        grad_up_weight,
        grad_up_bias,
        grad_down_weight,
        grad_down_bias,
    )


def solution(mesh):
    mesh = jax.sharding.Mesh(mesh.devices.reshape(SIZES), AXES)
    split, groups = P(("x", "zh"), SEQ, None), P(("x", "zh"), None)
    in_specs = (split, groups, groups, *(P(),) * 12, split)
    out_specs = (split, split, *(P(),) * 12)
    return jax.shard_map(body, mesh=mesh, in_specs=in_specs, out_specs=out_specs, check_vma=False)
```

time: 362 us -> 256 us (0.71)
  waiting for transfers between devices: 151 us -> 85.8 us
  Pallas kernels: 50.4 us -> 88.2 us
  starting transfers between devices: 60.8 us -> 34.2 us
  local copies, waits for them, and re-layouts: 37.8 us -> 14.8 us
  matrix products: 15.8 us -> 0 us
  other arithmetic: 30 us -> 15.3 us
    ppermute x18 -> x20, waiting for transfers between devices: 135 us -> 76.5 us  [swap(): return lax.ppermute(value, AXES, pairs)]
    pallas_call x0 -> x12, Pallas kernels: none -> 41.7 us  [the longest x2 20.3 us: feed_half(): pl.pallas_call(feed_kernel, out_shape=(jax.ShapeDtypeStruct((2, units, D)...]
    ppermute x18 -> x20, starting transfers between devices: 44.6 us -> 20.8 us  [swap(): return lax.ppermute(value, AXES, pairs)]
    dot_general x8 -> x0, matrix products: 15.8 us -> none  [contract(): lax.dot_general(left, right, (dims, ((), ())), preferred_element_type=F32)]
    all_to_all x1 -> x2, waiting for transfers between devices: 15.8 us -> 0.01 us  [the longest x1 0.01 us: body(): spread = lax.all_to_all(feed_sum, ('y', 'zl', 'zh'), 0, 0, tiled=True)]
    slice x8 -> x0, local copies, waits for them, and re-layouts: 11.3 us -> none  [the longest x1 3.65 us: body(): heads[:, 0:192].reshape(H, 3, DH, D).transpose(3, 1, 0, 2).reshape(D, 3 * D)]
    pallas_call x1, Pallas kernels: 37.6 us -> 27.2 us  [one_head(): pl.pallas_call(head_kernel, out_shape=(jax.ShapeDtypeStruct((SEQ_DEV, 256...]
    concatenate x11 -> x0, other arithmetic: 9.81 us -> none  [the longest x2 2.49 us: ring_gather(): value = jnp.concatenate([value, got], 0)]
  transfers between devices with their start and end apart: 21 -> 24, of which waited for: 14 -> 13; matrix products, arithmetic and copies ran while one was open for 9% -> 7% of each run, Pallas kernels for 14% -> 30%
where the time goes in v2:
time: 256 us; the launch traced here: 253 us
  Pallas kernels  88.2 us (34%)
  waiting for transfers between devices  85.8 us (34%)
  starting transfers between devices  34.2 us (13%)
  other arithmetic  15.3 us (6%)
  local copies, waits for them, and re-layouts  14.8 us (6%)
  between operations  14.3 us (6%)
    ppermute x20, waiting for transfers between devices, swap(): return lax.ppermute(value, AXES, pairs)  76.5 us
    pallas_call x1, Pallas kernels, one_head(): pl.pallas_call(head_kernel, out_shape=(jax.ShapeDtypeStruct((SEQ_DEV, 256...  27.2 us
    ppermute x20, starting transfers between devices, swap(): return lax.ppermute(value, AXES, pairs)  20.8 us
    pallas_call x2, Pallas kernels, feed_half(): pl.pallas_call(feed_kernel, out_shape=(jax.ShapeDtypeStruct((2, units, D)...  20.3 us
    pallas_call x4, Pallas kernels, place_feed(): pl.pallas_call(place_feed_kernel, out_shape=(jax.ShapeDtypeStruct((FF, D)...  19.3 us
    unnamed x48, local copies, waits for them, and re-layouts  11.2 us
    all_gather x1, waiting for transfers between devices, body(): sums = lax.all_gather(hold(head_sum, back, one, two), SEQ, axis=0)  8.76 us
    convert_element_type x6, other arithmetic, added(): return total.astype(BF16)  8.31 us
  transfers between devices with their start and end apart: 24, of which 13 were waited for; matrix products, arithmetic and copies ran while one was open for 7% of the time, Pallas kernels for 30%

profile of v2, /device:TPU:97, one launch (start us, length us, event | category | flops | bytes accessed | tf_op | source)
XLA Modules:
  0.0 252.6 jit_solution(9255225233513983252)
XLA Ops:
  7.2 3.0 %norms.1 = (bf16[256,1536]{1,0:T(8,128)(2,1)}, bf16[256,1536]{1,0:T(8,128)(2,1)}, f32[256,768]{1,0:T(8,128)}, f32[256,128]{1,0:T(8,128)}) custom-call(bf16[256,768]{1,0:T(8,128)(2,1)} %bitcast.41, bf16[256,768]{1,0:T(8,128)(2,1)} %bitcast.37, bf16[768]{0:T(1024)(128)(2,1)} %gain1_ref.3, bf16[768]{0:T(1024)(128)(2,1)} %shift1_ref.1, ...), custom_call_target="tpu_custom_call" | custom-call | flops 300000000 | bytes 5000000 | tf_op jit(solution)/shard_map/norms/pallas_call | solution.py:126
  14.0 9.6 %feed.2 = (bf16[2,768,768]{2,1,0:T(8,128)(2,1)}, f32[1,768]{1,0:T(1,128)}, f32[512,1536]{1,0:T(8,128)}) custom-call(s32[1]{0:T(128)} %bitcast.8.where, bf16[256,1536]{1,0:T(8,128)(2,1)} %get-tuple-element.49.own_ref, bf16[256,1536]{1,0:T(8,128)(2,1)} %copy-done.23, bf16[768,3072]{1,0:T(8,128)(2,1)} %up_ref.3, bf16[3072,768]{1,0:T(8,128)(2,1)} %down_ref.3, ...), custom_call_target="tpu_custom_call" | custom-call | flops 4000000000 | bytes 8000000 | tf_op jit(solution)/shard_map/feed/pallas_call | solution.py:479
  23.7 2.6 %collective-permute-start.2 = (bf16[2,768,768]{2,1,0:T(8,128)(2,1)}, bf16[2,768,768]{2,1,0:T(8,128)(2,1)S(1)}, u32[]{:S(2)}, u32[]{:S(2)}) collective-permute-start(bf16[2,768,768]{2,1,0:T(8,128)(2,1)} %get-tuple-element.57), channel_id=1, source_target_pairs={{0,2},{1,3},{2,0},{3,1},{4,6},{5,7},{6,4},{7,5},{8,14},{9,15},{10,... | collective-permute-start | bytes 7077896 | tf_op jit(solution)/shard_map/feed_scatter/ppermute | solution.py:51
  26.3 10.6 %feed.3 = (bf16[2,768,768]{2,1,0:T(8,128)(2,1)}, f32[1,768]{1,0:T(1,128)}, f32[256,1536]{1,0:T(8,128)}, bf16[256,1536]{1,0:T(8,128)(2,1)}) custom-call(s32[1]{0:T(128)} %bitcast.6.where, bf16[256,1536]{1,0:T(8,128)(2,1)} %get-tuple-element.49.own_ref, bf16[256,1536]{1,0:T(8,128)(2,1)} %copy-done.23, bf16[768,3072]{1,0:T(8,128)(2,1)} %up_ref.3, ...), custom_call_target="tpu_custom_call" | custom-call | flops 4000000000 | bytes 8000000 | tf_op jit(solution)/shard_map/feed/pallas_call | solution.py:479
  37.0 15.9 %collective-permute-done.2 = bf16[2,768,768]{2,1,0:T(8,128)(2,1)S(1)} collective-permute-done((bf16[2,768,768]{2,1,0:T(8,128)(2,1)}, bf16[2,768,768]{2,1,0:T(8,128)(2,1)S(1)}, u32[]{:S(2)}, u32[]{:S(2)}) %collective-permute-start.2) | collective-permute-done | bytes 2359328 | tf_op jit(solution)/shard_map/feed_scatter/ppermute | solution.py:51
  54.3 3.1 %add_convert_fusion = bf16[2,768,768]{2,1,0:T(8,128)(2,1)S(1)} fusion(bf16[2,768,768]{2,1,0:T(8,128)(2,1)} %copy-done.7, bf16[2,768,768]{2,1,0:T(8,128)(2,1)} %get-tuple-element.56), kind=kLoop, calls=%fused_computation | loop fusion | flops 4718592 | bytes 7077888 | tf_op jit(solution)/shard_map/feed_scatter/convert_element_type | solution.py:93
  60.9 1.9 convert_add_fusion.parts_ref
  64.7 9.4 %collective-permute-done.3 = bf16[2,384,768]{2,1,0:T(8,128)(2,1)} collective-permute-done((bf16[2,384,768]{2,1,0:T(8,128)(2,1)}, bf16[2,384,768]{2,1,0:T(8,128)(2,1)}, u32[]{:S(2)}, u32[]{:S(2)}) %collective-permute-start.3) | collective-permute-done | bytes 1179680 | tf_op jit(solution)/shard_map/feed_scatter/ppermute | solution.py:51
  74.2 1.6 add_convert_fusion.1
  76.8 6.6 %all-to-all-start = ((bf16[16,2,24,768]{3,2,1,0:T(8,128)(2,1)}), bf16[16,2,24,768]{3,2,1,0:T(8,128)(2,1)S(1)}, u32[]{:S(2)}, u32[]{:S(2)}) async-start(bf16[16,2,24,768]{3,2,1,0:T(8,128)(2,1)} %bitcast.33), calls=%async_computation | async-start | bytes 2359296 | tf_op jit(solution)/shard_map/feed_scatter/all_to_all | solution.py:778
  84.0 27.2 %head.1 = (bf16[16,256,256]{2,1,0:T(8,128)(2,1)}, bf16[272,768]{1,0:T(8,128)(2,1)}) custom-call(s32[4096]{0:T(1024)} %bitcast.46, s32[4096]{0:T(1024)} %bitcast.47, s32[2]{0:T(128)} %pad_add_fusion.which, bf16[4096,1536]{1,0:T(8,128)(2,1)} %all-gather.4.cloned.1.call-done.rows_hbm, f32[16,2048]{1,0:T(8,128)} %constant.42.clone.table_ref, ...), custom_call_target="tpu_custom_call" | custom-call | flops 24000000000 | bytes 12000000 | tf_op jit(solution)/shard_map/head/pallas_call | solution.py:367
  112.2 1.5 fusion.own_ref
  114.8 2.2 collective-permute-start.6
  120.0 1.8 rounds.6.own_ref
  123.0 2.0 collective-permute-start.8
  125.6 1.6 collective-permute-start.10
  127.5 6.4 %collective-permute-done.8.refs_1_ = bf16[2,96,768]{2,1,0:T(8,128)(2,1)S(1)} collective-permute-done((bf16[2,96,768]{2,1,0:T(8,128)(2,1)}, bf16[2,96,768]{2,1,0:T(8,128)(2,1)S(1)}, u32[]{:S(2)}, u32[]{:S(2)}) %collective-permute-start.8) | collective-permute-done | bytes 294944 | tf_op jit(solution)/shard_map/rounds/ppermute | solution.py:51
  133.9 5.6 %collective-permute-done.9.refs_2_ = bf16[2,96,768]{2,1,0:T(8,128)(2,1)S(1)} collective-permute-done((bf16[2,96,768]{2,1,0:T(8,128)(2,1)}, bf16[2,96,768]{2,1,0:T(8,128)(2,1)S(1)}, u32[]{:S(2)}, u32[]{:S(2)}) %collective-permute-start.9) | collective-permute-done | bytes 294944 | tf_op jit(solution)/shard_map/rounds/ppermute | solution.py:51
  140.3 2.4 rounds.7.refs_0_.value_ref
  142.7 6.7 %all-to-all-start.1 = ((bf16[16,256,256]{2,1,0:T(8,128)(2,1)}), bf16[16,256,256]{2,1,0:T(8,128)(2,1)S(1)}, u32[]{:S(2)}, u32[]{:S(2)}) async-start(bf16[16,256,256]{2,1,0:T(8,128)(2,1)} %rounds.8), calls=%async_computation.1 | async-start | bytes 4194304 | tf_op jit(solution)/shard_map/rounds/all_to_all | solution.py:819
  150.7 2.5 collective-permute-start.11
  154.1 7.2 %collective-permute-done.11 = bf16[272,768]{1,0:T(8,128)(2,1)S(1)} collective-permute-done((bf16[272,768]{1,0:T(8,128)(2,1)S(1)}, bf16[272,768]{1,0:T(8,128)(2,1)S(1)}, u32[]{:S(2)}, u32[]{:S(2)}) %collective-permute-start.11) | collective-permute-done | bytes 417824 | tf_op jit(solution)/shard_map/rounds/ppermute | solution.py:51
  162.4 26.2 %collective-permute-done.12 = bf16[272,768]{1,0:T(8,128)(2,1)S(1)} collective-permute-done((bf16[272,768]{1,0:T(8,128)(2,1)S(1)}, bf16[272,768]{1,0:T(8,128)(2,1)S(1)}, u32[]{:S(2)}, u32[]{:S(2)}) %collective-permute-start.12) | collective-permute-done | bytes 417824 | tf_op jit(solution)/shard_map/rounds/ppermute | solution.py:51
  193.1 2.4 collective-permute-start.15
  197.3 6.4 %heads_back.1 = (bf16[256,768]{1,0:T(8,128)(2,1)}, f32[256,768]{1,0:T(8,128)}) custom-call(bf16[16,256,256]{2,1,0:T(8,128)(2,1)} %copy-done.1, bf16[256,768]{1,0:T(8,128)(2,1)} %bitcast.42, bf16[256,768]{1,0:T(8,128)(2,1)} %bitcast.38, f32[256,768]{1,0:T(8,128)} %get-tuple-element.53.normal_ref, f32[256,128]{1,0:T(8,128)} %get-tuple-element.61.rate_ref, ...), custom_call_target="tpu_custom_call" | custom-call | tf_op jit(solution)/shard_map/heads_back/pallas_call | solution.py:699
  203.8 4.8 %feed_gather.7 = (f32[3072,768]{1,0:T(8,128)}, f32[768,3072]{1,0:T(8,128)}) custom-call(s32[2]{0:T(128)} %pad_add_fusion.4.where, bf16[2,384,768]{2,1,0:T(8,128)(2,1)} %feed_gather.6.mine_ref, bf16[2,384,768]{2,1,0:T(8,128)(2,1)} %collective-permute-done.18.theirs_ref), custom_call_target="tpu_custom_call" | custom-call | tf_op jit(solution)/shard_map/feed_gather/pallas_call | solution.py:585
  208.6 4.9 %feed_gather.8 = (f32[3072,768]{1,0:T(8,128)}, f32[768,3072]{1,0:T(8,128)}) custom-call(s32[2]{0:T(128)} %pad_add_fusion.3.where, bf16[2,384,768]{2,1,0:T(8,128)(2,1)} %copy-done.5, bf16[2,384,768]{2,1,0:T(8,128)(2,1)} %collective-permute-done.17.theirs_ref, f32[3072,768]{1,0:T(8,128)} %get-tuple-element.72.refs_0_, ...), custom_call_target="tpu_custom_call", output_to_operand_aliasing={{0}: (3, {}), {1}: (4, {})} | custom-call | tf_op jit(solution)/shard_map/feed_gather/pallas_call | solution.py:585
  214.4 4.8 %feed_gather.9 = (f32[3072,768]{1,0:T(8,128)}, f32[768,3072]{1,0:T(8,128)}) custom-call(s32[2]{0:T(128)} %pad_add_fusion.2.where, bf16[2,384,768]{2,1,0:T(8,128)(2,1)} %collective-permute-done.14.refs_2_.mine_ref, bf16[2,384,768]{2,1,0:T(8,128)(2,1)} %copy-done.9, ...), custom_call_target="tpu_custom_call", output_to_operand_aliasing={{0}: (3, {}), {1}: (4, {})} | custom-call | tf_op jit(solution)/shard_map/feed_gather/pallas_call | solution.py:585
  220.9 2.5 collective-permute-done.19.theirs_ref
  224.3 4.8 %feed_gather.11 = (f32[3072,768]{1,0:T(8,128)}, f32[768,3072]{1,0:T(8,128)}) custom-call(s32[2]{0:T(128)} %pad_add_fusion.1.where, bf16[2,384,768]{2,1,0:T(8,128)(2,1)} %feed_gather.10.mine_ref, bf16[2,384,768]{2,1,0:T(8,128)(2,1)} %copy-done.10, f32[3072,768]{1,0:T(8,128)} %get-tuple-element.76.refs_0_, ...), custom_call_target="tpu_custom_call", output_to_operand_aliasing={{0}: (3, {}), {1}: (4, {})} | custom-call | tf_op jit(solution)/shard_map/feed_gather/pallas_call | solution.py:585
  229.2 8.8 %all-gather.6.cloned.1.call-done = bf16[4352,768]{1,0:T(8,128)(2,1)} async-done(((bf16[272,768]{1,0:T(8,128)(2,1)}), bf16[4352,768]{1,0:T(8,128)(2,1)}) %all-gather.6.cloned.1.call-update) | async-done | bytes 6684688 | tf_op jit(solution)/shard_map/rounds/all_gather | solution.py:824
  237.9 7.8 %head_place.1 = (f32[768,2304]{1,0:T(8,128)}, f32[768,768]{1,0:T(8,128)}, f32[768]{0:T(1024)}, f32[768]{0:T(1024)}, f32[2304]{0:T(1024)}, /*index=5*/f32[768]{0:...) custom-call(bf16[16,272,768]{2,1,0:T(8,128)(2,1)} %bitcast.34, bf16[16,272,768]{2,1,0:T(8,128)(2,1)} %bitcast.35), custom_call_target="tpu_custom_call" | custom-call | tf_op jit(solution)/shard_map/head_place/pallas_call | solution.py:640
  (111 shorter events, 33.5 us)
Async XLA Ops:
  7.2 76.8 %all-gather.4.cloned.1.call-start = ((), (), s32[]{:S(2)}) async-start(), calls=%async_computation.2 | async-start | bytes 13369344 | tf_op jit(solution)/shard_map/gather_rows/all_gather | solution.py:749
  10.2 2.9 %collective-permute-start = (bf16[256,1536]{1,0:T(8,128)(2,1)}, bf16[256,1536]{1,0:T(8,128)(2,1)S(1)}, u32[]{:S(2)}, u32[]{:S(2)}) collective-permute-start(bf16[256,1536]{1,0:T(8,128)(2,1)} %get-tuple-element.49.own_ref), channel_id=1, source_target_pairs={{0,8},{1,9},{2,10},{3,11},{4,12},{5,13},{6,14},{7,15},{8,0},{9,1},... | collective-permute-start | bytes 2359304 | tf_op jit(solution)/shard_map/feed/ppermute | solution.py:51
  14.0 12.2 %copy-start.18 = (bf16[768]{0:T(1024)(128)(2,1)S(1)}, bf16[768]{0:T(1024)(128)(2,1)}, u32[]{:S(2)}) copy-start(bf16[768]{0:T(1024)(128)(2,1)} %gain1_ref.3) | copy-start | bytes 4612
  14.0 12.2 %copy-start.22 = (bf16[768]{0:T(1024)(128)(2,1)S(1)}, bf16[768]{0:T(1024)(128)(2,1)}, u32[]{:S(2)}) copy-start(bf16[768]{0:T(1024)(128)(2,1)} %shift1_ref.1) | copy-start | bytes 4612
  23.7 29.2 %collective-permute-start.2 = (bf16[2,768,768]{2,1,0:T(8,128)(2,1)}, bf16[2,768,768]{2,1,0:T(8,128)(2,1)S(1)}, u32[]{:S(2)}, u32[]{:S(2)}) collective-permute-start(bf16[2,768,768]{2,1,0:T(8,128)(2,1)} %get-tuple-element.57), channel_id=1, source_target_pairs={{0,2},{1,3},{2,0},{3,1},{4,6},{5,7},{6,4},{7,5},{8,14},{9,15},{10,... | collective-permute-start | bytes 7077896 | tf_op jit(solution)/shard_map/feed_scatter/ppermute | solution.py:51
  36.9 23.9 %collective-permute-start.1 = (bf16[256,1536]{1,0:T(8,128)(2,1)}, bf16[256,1536]{1,0:T(8,128)(2,1)}, u32[]{:S(2)}, u32[]{:S(2)}) collective-permute-start(bf16[256,1536]{1,0:T(8,128)(2,1)} %get-tuple-element.52), channel_id=1, source_target_pairs={{0,8},{1,9},{2,10},{3,11},{4,12},{5,13},{6,14},{7,15},{8,0},{9,1},... | collective-permute-start | bytes 2359304 | tf_op jit(solution)/shard_map/feed/ppermute | solution.py:51
  57.4 3.5 %copy-start.20 = (f32[1,768]{1,0:T(1,128)S(1)}, f32[1,768]{1,0:T(1,128)}, u32[]{:S(2)}) copy-start(f32[1,768]{1,0:T(1,128)} %get-tuple-element.55) | copy-start | bytes 9220
  58.5 5.4 %copy-start.6 = (f32[256,768]{1,0:T(8,128)S(1)}, f32[256,768]{1,0:T(8,128)}, u32[]{:S(2)}) copy-start(f32[256,768]{1,0:T(8,128)} %get-tuple-element.53.normal_ref) | copy-start | bytes 2359300
  58.5 15.7 %collective-permute-start.3 = (bf16[2,384,768]{2,1,0:T(8,128)(2,1)}, bf16[2,384,768]{2,1,0:T(8,128)(2,1)}, u32[]{:S(2)}, u32[]{:S(2)}) collective-permute-start(bf16[2,384,768]{2,1,0:T(8,128)(2,1)} %constant_dynamic-slice_fusion), channel_id=1, source_target_pairs={{0,6},{1,7},{2,4},{3,5},{4,2},{5,3},{6,0},{7,1},{8,10},{9,11},{10,... | collective-permute-start | bytes 3538952 | tf_op jit(solution)/shard_map/feed_scatter/ppermute | solution.py:51
  76.8 34.4 %all-to-all-start = ((bf16[16,2,24,768]{3,2,1,0:T(8,128)(2,1)}), bf16[16,2,24,768]{3,2,1,0:T(8,128)(2,1)S(1)}, u32[]{:S(2)}, u32[]{:S(2)}) async-start(bf16[16,2,24,768]{3,2,1,0:T(8,128)(2,1)} %bitcast.33), calls=%async_computation | async-start | bytes 2359296 | tf_op jit(solution)/shard_map/feed_scatter/all_to_all | solution.py:778
  113.7 5.6 %copy-start.14 = (bf16[2,24,768]{2,1,0:T(8,128)(2,1)}, bf16[2,24,768]{2,1,0:T(8,128)(2,1)S(1)}, u32[]{:S(2)}) copy-start(bf16[2,24,768]{2,1,0:T(8,128)(2,1)S(1)} %fusion.own_ref) | copy-start | bytes 221188
  113.7 4.8 %collective-permute-start.4 = (bf16[2,24,768]{2,1,0:T(8,128)(2,1)S(1)}, bf16[2,24,768]{2,1,0:T(8,128)(2,1)S(1)}, u32[]{:S(2)}, u32[]{:S(2)}) collective-permute-start(bf16[2,24,768]{2,1,0:T(8,128)(2,1)S(1)} %fusion.own_ref), channel_id=1, source_target_pairs={{0,1},{1,0},{2,3},{3,2},{4,5},{5,4},{6,7},{7,6},{8,9},{9,8},{10,11... | collective-permute-start | bytes 221192 | tf_op jit(solution)/shard_map/rounds/ppermute | solution.py:51
  114.8 3.7 %collective-permute-start.5 = (bf16[2,24,768]{2,1,0:T(8,128)(2,1)S(1)}, bf16[2,24,768]{2,1,0:T(8,128)(2,1)S(1)}, u32[]{:S(2)}, u32[]{:S(2)}) collective-permute-start(bf16[2,24,768]{2,1,0:T(8,128)(2,1)S(1)} %fusion.own_ref), channel_id=1, source_target_pairs={{0,16},{1,17},{2,18},{3,19},{4,20},{5,21},{6,22},{7,23},{8,24},{9,... | collective-permute-start | bytes 221192 | tf_op jit(solution)/shard_map/rounds/ppermute | solution.py:51
  114.8 4.5 %collective-permute-start.6 = (bf16[2,24,768]{2,1,0:T(8,128)(2,1)S(1)}, bf16[2,24,768]{2,1,0:T(8,128)(2,1)S(1)}, u32[]{:S(2)}, u32[]{:S(2)}) collective-permute-start(bf16[2,24,768]{2,1,0:T(8,128)(2,1)S(1)} %fusion.own_ref), channel_id=1, source_target_pairs={{0,17},{1,16},{2,19},{3,18},{4,21},{5,20},{6,23},{7,22},{8,25},{9,... | collective-permute-start | bytes 221192 | tf_op jit(solution)/shard_map/rounds/ppermute | solution.py:51
  121.8 5.8 %collective-permute-start.7 = (bf16[2,96,768]{2,1,0:T(8,128)(2,1)}, bf16[2,96,768]{2,1,0:T(8,128)(2,1)S(1)}, u32[]{:S(2)}, u32[]{:S(2)}) collective-permute-start(bf16[2,96,768]{2,1,0:T(8,128)(2,1)} %rounds.6.own_ref), channel_id=1, source_target_pairs={{0,32},{1,33},{2,34},{3,35},{4,36},{5,37},{6,38},{7,39},{8,40},{9,... | collective-permute-start | bytes 884744 | tf_op jit(solution)/shard_map/rounds/ppermute | solution.py:51
  123.0 11.0 %collective-permute-start.8 = (bf16[2,96,768]{2,1,0:T(8,128)(2,1)}, bf16[2,96,768]{2,1,0:T(8,128)(2,1)S(1)}, u32[]{:S(2)}, u32[]{:S(2)}) collective-permute-start(bf16[2,96,768]{2,1,0:T(8,128)(2,1)} %rounds.6.own_ref), channel_id=1, source_target_pairs={{0,64},{1,65},{2,66},{3,67},{4,68},{5,69},{6,70},{7,71},{8,72},{9,... | collective-permute-start | bytes 884744 | tf_op jit(solution)/shard_map/rounds/ppermute | solution.py:51
  124.9 14.6 %collective-permute-start.9 = (bf16[2,96,768]{2,1,0:T(8,128)(2,1)}, bf16[2,96,768]{2,1,0:T(8,128)(2,1)S(1)}, u32[]{:S(2)}, u32[]{:S(2)}) collective-permute-start(bf16[2,96,768]{2,1,0:T(8,128)(2,1)} %rounds.6.own_ref), channel_id=1, source_target_pairs={{0,96},{1,97},{2,98},{3,99},{4,100},{5,101},{6,102},{7,103},{8,104... | collective-permute-start | bytes 884744 | tf_op jit(solution)/shard_map/rounds/ppermute | solution.py:51
  125.6 23.8 %collective-permute-start.10 = (bf16[272,768]{1,0:T(8,128)(2,1)}, bf16[272,768]{1,0:T(8,128)(2,1)}, u32[]{:S(2)}, u32[]{:S(2)}) collective-permute-start(bf16[272,768]{1,0:T(8,128)(2,1)} %get-tuple-element.60.refs_0_), channel_id=1, source_target_pairs={{0,1},{1,0},{2,3},{3,2},{4,5},{5,4},{6,7},{7,6},{8,9},{9,8},{10,11... | collective-permute-start | bytes 1253384 | tf_op jit(solution)/shard_map/rounds/ppermute | solution.py:51
  127.5 12.0 %copy-start.11 = (bf16[2,96,768]{2,1,0:T(8,128)(2,1)}, bf16[2,96,768]{2,1,0:T(8,128)(2,1)S(1)}, u32[]{:S(2)}) copy-start(bf16[2,96,768]{2,1,0:T(8,128)(2,1)S(1)} %collective-permute-done.7.refs_0_) | copy-start | bytes 884740
  133.9 5.6 %copy-start.12 = (bf16[2,96,768]{2,1,0:T(8,128)(2,1)}, bf16[2,96,768]{2,1,0:T(8,128)(2,1)S(1)}, u32[]{:S(2)}) copy-start(bf16[2,96,768]{2,1,0:T(8,128)(2,1)S(1)} %collective-permute-done.8.refs_1_) | copy-start | bytes 884740
  142.7 10.5 %copy-start = (bf16[2,384,768]{2,1,0:T(8,128)(2,1)S(1)}, bf16[2,384,768]{2,1,0:T(8,128)(2,1)}, u32[]{:S(2)}) copy-start(bf16[2,384,768]{2,1,0:T(8,128)(2,1)} %rounds.7.refs_0_.value_ref) | copy-start | bytes 3538948
  142.7 47.8 %all-to-all-start.1 = ((bf16[16,256,256]{2,1,0:T(8,128)(2,1)}), bf16[16,256,256]{2,1,0:T(8,128)(2,1)S(1)}, u32[]{:S(2)}, u32[]{:S(2)}) async-start(bf16[16,256,256]{2,1,0:T(8,128)(2,1)} %rounds.8), calls=%async_computation.1 | async-start | bytes 4194304 | tf_op jit(solution)/shard_map/rounds/all_to_all | solution.py:819
  149.4 88.5 %all-gather.6.cloned.1.call-start = ((), (), s32[]{:S(2)}) async-start(), calls=%async_computation.3 | async-start | bytes 7102464 | tf_op jit(solution)/shard_map/rounds/all_gather | solution.py:824
  150.7 10.6 %collective-permute-start.11 = (bf16[272,768]{1,0:T(8,128)(2,1)S(1)}, bf16[272,768]{1,0:T(8,128)(2,1)S(1)}, u32[]{:S(2)}, u32[]{:S(2)}) collective-permute-start(bf16[272,768]{1,0:T(8,128)(2,1)S(1)} %add_convert_fusion.4), channel_id=1, source_target_pairs={{0,2},{1,3},{2,0},{3,1},{4,6},{5,7},{6,4},{7,5},{8,14},{9,15},{10,... | collective-permute-start | bytes 1253384 | tf_op jit(solution)/shard_map/rounds/ppermute | solution.py:51
  153.2 36.2 %collective-permute-start.13 = (bf16[2,384,768]{2,1,0:T(8,128)(2,1)S(1)}, bf16[2,384,768]{2,1,0:T(8,128)(2,1)S(1)}, u32[]{:S(2)}, u32[]{:S(2)}) collective-permute-start(bf16[2,384,768]{2,1,0:T(8,128)(2,1)S(1)} %copy-done), channel_id=1, source_target_pairs={{0,6},{1,7},{2,4},{3,5},{4,2},{5,3},{6,0},{7,1},{8,10},{9,11},{10,... | collective-permute-start | bytes 3538952 | tf_op jit(solution)/shard_map/rounds/ppermute | solution.py:51
  153.2 37.2 %collective-permute-start.14 = (bf16[2,384,768]{2,1,0:T(8,128)(2,1)S(1)}, bf16[2,384,768]{2,1,0:T(8,128)(2,1)}, u32[]{:S(2)}, u32[]{:S(2)}) collective-permute-start(bf16[2,384,768]{2,1,0:T(8,128)(2,1)S(1)} %copy-done), channel_id=1, source_target_pairs={{0,2},{1,3},{2,0},{3,1},{4,6},{5,7},{6,4},{7,5},{8,14},{9,15},{10,... | collective-permute-start | bytes 3538952 | tf_op jit(solution)/shard_map/rounds/ppermute | solution.py:51
  161.3 27.2 %collective-permute-start.12 = (bf16[272,768]{1,0:T(8,128)(2,1)S(1)}, bf16[272,768]{1,0:T(8,128)(2,1)S(1)}, u32[]{:S(2)}, u32[]{:S(2)}) collective-permute-start(bf16[272,768]{1,0:T(8,128)(2,1)S(1)} %add_convert_fusion.3), channel_id=1, source_target_pairs={{0,6},{1,7},{2,4},{3,5},{4,2},{5,3},{6,0},{7,1},{8,10},{9,11},{10,... | collective-permute-start | bytes 1253384 | tf_op jit(solution)/shard_map/rounds/ppermute | solution.py:51
  191.8 12.0 %collective-permute-start.18 = (bf16[2,384,768]{2,1,0:T(8,128)(2,1)S(1)}, bf16[2,384,768]{2,1,0:T(8,128)(2,1)}, u32[]{:S(2)}, u32[]{:S(2)}) collective-permute-start(bf16[2,384,768]{2,1,0:T(8,128)(2,1)S(1)} %copy-done), channel_id=1, source_target_pairs={{0,8},{1,9},{2,10},{3,11},{4,12},{5,13},{6,14},{7,15},{8,0},{9,1},... | collective-permute-start | bytes 3538952 | tf_op jit(solution)/shard_map/feed_gather/ppermute | solution.py:51
  192.6 15.9 %collective-permute-start.17 = (bf16[2,384,768]{2,1,0:T(8,128)(2,1)}, bf16[2,384,768]{2,1,0:T(8,128)(2,1)}, u32[]{:S(2)}, u32[]{:S(2)}) collective-permute-start(bf16[2,384,768]{2,1,0:T(8,128)(2,1)} %copy-done.5), channel_id=1, source_target_pairs={{0,8},{1,9},{2,10},{3,11},{4,12},{5,13},{6,14},{7,15},{8,0},{9,1},... | collective-permute-start | bytes 3538952 | tf_op jit(solution)/shard_map/feed_gather/ppermute | solution.py:51
  192.7 20.7 %collective-permute-start.16 = (bf16[2,384,768]{2,1,0:T(8,128)(2,1)}, bf16[2,384,768]{2,1,0:T(8,128)(2,1)S(1)}, u32[]{:S(2)}, u32[]{:S(2)}) collective-permute-start(bf16[2,384,768]{2,1,0:T(8,128)(2,1)} %collective-permute-done.14.refs_2_.mine_ref), channel_id=1, source_target_pairs={{0,8},{1,9},{2,10},{3,11},{4,12},{5,13},{6,14},{7,15},{8,0},{9,1},... | collective-permute-start | bytes 3538952 | tf_op jit(solution)/shard_map/feed_gather/ppermute | solution.py:51
  193.1 26.1 %collective-permute-start.15 = (bf16[2,384,768]{2,1,0:T(8,128)(2,1)}, bf16[2,384,768]{2,1,0:T(8,128)(2,1)S(1)}, u32[]{:S(2)}, u32[]{:S(2)}) collective-permute-start(bf16[2,384,768]{2,1,0:T(8,128)(2,1)} %copy-done.5), channel_id=1, source_target_pairs={{0,2},{1,3},{2,0},{3,1},{4,6},{5,7},{6,4},{7,5},{8,14},{9,15},{10,... | collective-permute-start | bytes 3538952 | tf_op jit(solution)/shard_map/feed_gather/ppermute | solution.py:51
  220.3 3.1 %collective-permute-start.19 = (bf16[2,384,768]{2,1,0:T(8,128)(2,1)}, bf16[2,384,768]{2,1,0:T(8,128)(2,1)S(1)}, u32[]{:S(2)}, u32[]{:S(2)}) collective-permute-start(bf16[2,384,768]{2,1,0:T(8,128)(2,1)} %feed_gather.10.mine_ref), channel_id=1, source_target_pairs={{0,8},{1,9},{2,10},{3,11},{4,12},{5,13},{6,14},{7,15},{8,0},{9,1},... | collective-permute-start | bytes 3538952 | tf_op jit(solution)/shard_map/feed_gather/ppermute | solution.py:51
  (16 other events, 20.1 us)
Sparse Core Ops, SparseCore 0:
  10.4 73.5 all-gather.3
  191.9 46.0 all-gather.5

commit v3 on v2

--- a/solution.py
+++ b/solution.py
@@ -544,6 +544,13 @@
     )(value, *later)
 
 
+def total_of(*refs):
+    total = refs[0][...].astype(F32)
+    for ref in refs[1:]:
+        total = total + ref[...].astype(F32)
+    return total.astype(BF16)
+
+
 def quad_kernel(which, own_ref, *refs):
     values = [own_ref[...].astype(F32), *[ref[...].astype(F32) for ref in refs[:3]]]
     rows = []
@@ -552,14 +559,16 @@
         for r in range(3):
             row = jnp.where((which[0] ^ k) == r, values[r], row)
         rows.append(row)
-    refs[-1][...] = jnp.concatenate(rows, 1).astype(BF16)
+    refs[-2][...] = jnp.concatenate(rows, 1).astype(BF16)
+    refs[-1][...] = total_of(*refs[3:5])
 
 
 def line_kernel(which, own_ref, *refs):
     rows = own_ref.shape[1]
     for r, ref in enumerate((own_ref, *refs[:3])):
         to = pl.multiple_of((which[0] ^ r) * rows, rows)
-        refs[-1][:, pl.ds(to, rows), :] = ref[...]
+        refs[-2][:, pl.ds(to, rows), :] = ref[...]
+    refs[-1][...] = total_of(*refs[3:7])
 
 
 def place_feed_kernel(where, mine_ref, theirs_ref, *refs):
@@ -598,7 +607,7 @@
             ),
         ),
         input_output_aliases={3: 0, 4: 1} if placed else {},
-        cost_estimate=pl.CostEstimate(flops=0, bytes_accessed=0, transcendentals=0),
+        cost_estimate=pl.CostEstimate(flops=0, bytes_accessed=7 * 10**6, transcendentals=0),
     )(where, mine, theirs, *placed)
 
 
@@ -800,47 +809,56 @@
         def flipped(*axes):
             return lambda p: {**p, **{axis: 1 - p[axis] for axis in axes}}
 
-        def along_y(r):
-            return lambda p: {**p, "y": p["y"] ^ r}
-
-        spread = hold(spread, head_sum)
+        def along(axis, r):
+            return lambda p: {**p, axis: p[axis] ^ r}
+
+        head_sum = hold(head_sum, spread)
         feed_sum = added(*[spread[n] for n in range(16)])
-        (feed_sum,) = round_call(
+        feed_sum, head_sum = round_call(
             quad_kernel,
             scalars(at["zl"] * 2 + at["zh"]),
-            (feed_sum, *[swap(feed_sum, flipped(*f)) for f in (("zh",), ("zl",), ("zl", "zh"))]),
-            ((2, 96, D),),
-        )
-        head_sum = added(head_sum, swap(head_sum, other("zh")))
-        got = [swap(feed_sum, along_y(r)) for r in (1, 2, 3)]
-        (feed_sum,) = round_call(
-            line_kernel, scalars(at["y"]), (feed_sum, *got), ((2, FF // 8, D),)
+            (
+                feed_sum,
+                *[swap(feed_sum, flipped(*f)) for f in (("zh",), ("zl",), ("zl", "zh"))],
+                head_sum,
+                swap(head_sum, flipped("zh")),
+            ),
+            ((2, 96, D), (HEAD_ROWS, D)),
+        )
+        feed_sum, head_sum = round_call(
+            line_kernel,
+            scalars(at["y"]),
+            (
+                feed_sum,
+                *[swap(feed_sum, along("y", r)) for r in (1, 2, 3)],
+                head_sum,
+                *[swap(head_sum, along("x", r)) for r in (1, 2, 3)],
+            ),
+            ((2, FF // 8, D), (HEAD_ROWS, D)),
         )
         back = lax.all_to_all(hold(send, feed_sum), SEQ, 0, 0, tiled=True)
-        for step in range(2):
-            head_sum = added(head_sum, swap(head_sum, ring_partner("x", step)))
         one = swap(feed_sum, ring_partner("x", 1))
         two = swap(feed_sum, ring_partner("x", 0))
-        sums = lax.all_gather(hold(head_sum, back, one, two), SEQ, axis=0)
-
-    with jax.named_scope("heads_back"):
-        result, grad_tokens = finish(
-            back, tokens[0], grad_rows, normal, rate, parts, first_gain, second_gain,
-            output_bias, down_bias, output_weight, input_weight,
-        )
-        result, grad_tokens = result[None], grad_tokens[None]
+        sums = lax.all_gather(head_sum, SEQ, axis=0)
 
     with jax.named_scope("feed_gather"):
         blocks = [
             [c * 4 + ring_chunk(x, c) for x in ring_slots(at["x"], c)] for c in (core, 1 - core)
         ]
         where = [scalars(blocks[0][n], blocks[1][n]) for n in range(4)]
+        theirs = swap(feed_sum, other("c"))
+        placed = place_feed(where[0], feed_sum, theirs, ())
+        one = hold(one, placed[0])
         last = swap(one, ring_partner("x", 0))
-        theirs = swap(feed_sum, other("c"))
-        placed = place_feed(where[0], hold(feed_sum, grad_tokens), theirs, ())
         placed = place_feed(where[1], one, swap(one, other("c")), placed)
         placed = place_feed(where[2], two, swap(two, other("c")), placed)
-        last = hold(last, placed[0])
+        with jax.named_scope("heads_back"):
+            result, grad_tokens = finish(
+                hold(back, placed[0], last), tokens[0], grad_rows, normal, rate, parts, first_gain, second_gain,
+                output_bias, down_bias, output_weight, input_weight,
+            )
+            result, grad_tokens = result[None], grad_tokens[None]
+        last = hold(last, grad_tokens)
         placed = place_feed(where[3], last, swap(last, other("c")), placed)
         grad_down_weight, grad_up_weight = placed
 

time: 256 us -> 251 us (0.980)
  waiting for transfers between devices: 85.8 us -> 80.2 us
    all_to_all x1, waiting for transfers between devices: 0.01 us -> 8.92 us  [body(): back = lax.all_to_all(hold(send, feed_sum), SEQ, 0, 0, tiled=True)]
    all_gather x1, waiting for transfers between devices: 8.76 us -> 0.01 us  [body(): sums = lax.all_gather(head_sum, SEQ, axis=0)]
    ppermute x20 -> x21, waiting for transfers between devices: 76.5 us -> 70.7 us  [swap(): return lax.ppermute(value, AXES, pairs)]
    ppermute x20 -> x21, starting transfers between devices: 20.8 us -> 24.7 us  [swap(): return lax.ppermute(value, AXES, pairs)]
    convert_element_type x6 -> x3, other arithmetic: 8.31 us -> 6.12 us  [added(): return total.astype(BF16)]
    unnamed x48 -> x52, local copies, waits for them, and re-layouts: 11.2 us -> 9.94 us
  transfers between devices with their start and end apart: 24 -> 25, of which waited for: 13 -> 14; matrix products, arithmetic and copies ran while one was open for 7% -> 7% of each run, Pallas kernels for 30% -> 30%
where the time goes in v3:
time: 251 us; the launch traced here: 247 us
  Pallas kernels  89.4 us (36%)
  waiting for transfers between devices  80.2 us (32%)
  starting transfers between devices  36.1 us (14%)
  between operations  14.4 us (6%)
  local copies, waits for them, and re-layouts  13.5 us (5%)
  other arithmetic  13.1 us (5%)
    ppermute x21, waiting for transfers between devices, swap(): return lax.ppermute(value, AXES, pairs)  70.7 us
    pallas_call x1, Pallas kernels, one_head(): pl.pallas_call(head_kernel, out_shape=(jax.ShapeDtypeStruct((SEQ_DEV, 256...  27.3 us
    ppermute x21, starting transfers between devices, swap(): return lax.ppermute(value, AXES, pairs)  24.7 us
    pallas_call x2, Pallas kernels, feed_half(): pl.pallas_call(feed_kernel, out_shape=(jax.ShapeDtypeStruct((2, units, D)...  20.3 us
    pallas_call x4, Pallas kernels, place_feed(): pl.pallas_call(place_feed_kernel, out_shape=(jax.ShapeDtypeStruct((FF, D)...  19.2 us
    unnamed x52, local copies, waits for them, and re-layouts  9.94 us
    all_to_all x1, waiting for transfers between devices, body(): back = lax.all_to_all(hold(send, feed_sum), SEQ, 0, 0, tiled=True)  8.92 us
    pallas_call x1, Pallas kernels, place_heads(): pl.pallas_call(place_heads_kernel, out_shape=(jax.ShapeDtypeStruct((D, 3...  7.81 us
  transfers between devices with their start and end apart: 25, of which 14 were waited for; matrix products, arithmetic and copies ran while one was open for 7% of the time, Pallas kernels for 30%

profile of v3, /device:TPU:97, one launch (start us, length us, event | category | flops | bytes accessed | tf_op | source)
XLA Modules:
  0.0 246.6 jit_solution(10105448243744598448)
XLA Ops:
  7.2 3.0 %norms.1 = (bf16[256,1536]{1,0:T(8,128)(2,1)}, bf16[256,1536]{1,0:T(8,128)(2,1)}, f32[256,768]{1,0:T(8,128)}, f32[256,128]{1,0:T(8,128)}) custom-call(bf16[256,768]{1,0:T(8,128)(2,1)} %bitcast.41, bf16[256,768]{1,0:T(8,128)(2,1)} %bitcast.37, bf16[768]{0:T(1024)(128)(2,1)} %gain1_ref.3, bf16[768]{0:T(1024)(128)(2,1)} %shift1_ref.1, ...), custom_call_target="tpu_custom_call" | custom-call | flops 300000000 | bytes 5000000 | tf_op jit(solution)/shard_map/norms/pallas_call | solution.py:126
  14.0 9.6 %feed.2 = (bf16[2,768,768]{2,1,0:T(8,128)(2,1)}, f32[1,768]{1,0:T(1,128)}, f32[512,1536]{1,0:T(8,128)}) custom-call(s32[1]{0:T(128)} %bitcast.8.where, bf16[256,1536]{1,0:T(8,128)(2,1)} %get-tuple-element.53.own_ref, bf16[256,1536]{1,0:T(8,128)(2,1)} %copy-done.25, bf16[768,3072]{1,0:T(8,128)(2,1)} %up_ref.3, bf16[3072,768]{1,0:T(8,128)(2,1)} %down_ref.3, ...), custom_call_target="tpu_custom_call" | custom-call | flops 4000000000 | bytes 8000000 | tf_op jit(solution)/shard_map/feed/pallas_call | solution.py:479
  23.6 2.6 %collective-permute-start.2 = (bf16[2,768,768]{2,1,0:T(8,128)(2,1)}, bf16[2,768,768]{2,1,0:T(8,128)(2,1)S(1)}, u32[]{:S(2)}, u32[]{:S(2)}) collective-permute-start(bf16[2,768,768]{2,1,0:T(8,128)(2,1)} %get-tuple-element.61), channel_id=1, source_target_pairs={{0,2},{1,3},{2,0},{3,1},{4,6},{5,7},{6,4},{7,5},{8,14},{9,15},{10,... | collective-permute-start | bytes 7077896 | tf_op jit(solution)/shard_map/feed_scatter/ppermute | solution.py:51
  26.2 10.6 %feed.3 = (bf16[2,768,768]{2,1,0:T(8,128)(2,1)}, f32[1,768]{1,0:T(1,128)}, f32[256,1536]{1,0:T(8,128)}, bf16[256,1536]{1,0:T(8,128)(2,1)}) custom-call(s32[1]{0:T(128)} %bitcast.6.where, bf16[256,1536]{1,0:T(8,128)(2,1)} %get-tuple-element.53.own_ref, bf16[256,1536]{1,0:T(8,128)(2,1)} %copy-done.25, bf16[768,3072]{1,0:T(8,128)(2,1)} %up_ref.3, ...), custom_call_target="tpu_custom_call" | custom-call | flops 4000000000 | bytes 8000000 | tf_op jit(solution)/shard_map/feed/pallas_call | solution.py:479
  37.0 15.9 %collective-permute-done.2 = bf16[2,768,768]{2,1,0:T(8,128)(2,1)S(1)} collective-permute-done((bf16[2,768,768]{2,1,0:T(8,128)(2,1)}, bf16[2,768,768]{2,1,0:T(8,128)(2,1)S(1)}, u32[]{:S(2)}, u32[]{:S(2)}) %collective-permute-start.2) | collective-permute-done | bytes 2359328 | tf_op jit(solution)/shard_map/feed_scatter/ppermute | solution.py:51
  54.2 3.1 %add_convert_fusion = bf16[2,768,768]{2,1,0:T(8,128)(2,1)S(1)} fusion(bf16[2,768,768]{2,1,0:T(8,128)(2,1)} %copy-done.6, bf16[2,768,768]{2,1,0:T(8,128)(2,1)} %get-tuple-element.60), kind=kLoop, calls=%fused_computation | loop fusion | flops 4718592 | bytes 7077888 | tf_op jit(solution)/shard_map/feed_scatter/convert_element_type | solution.py:93
  60.8 1.9 convert_add_fusion.parts_ref
  64.7 9.4 %collective-permute-done.3 = bf16[2,384,768]{2,1,0:T(8,128)(2,1)} collective-permute-done((bf16[2,384,768]{2,1,0:T(8,128)(2,1)}, bf16[2,384,768]{2,1,0:T(8,128)(2,1)}, u32[]{:S(2)}, u32[]{:S(2)}) %collective-permute-start.3) | collective-permute-done | bytes 1179680 | tf_op jit(solution)/shard_map/feed_scatter/ppermute | solution.py:51
  76.8 6.6 %all-to-all-start = ((bf16[16,2,24,768]{3,2,1,0:T(8,128)(2,1)}), bf16[16,2,24,768]{3,2,1,0:T(8,128)(2,1)S(1)}, u32[]{:S(2)}, u32[]{:S(2)}) async-start(bf16[16,2,24,768]{3,2,1,0:T(8,128)(2,1)} %bitcast.33), calls=%async_computation | async-start | bytes 2359296 | tf_op jit(solution)/shard_map/feed_scatter/all_to_all | solution.py:787
  83.9 27.3 %head.1 = (bf16[16,256,256]{2,1,0:T(8,128)(2,1)}, bf16[272,768]{1,0:T(8,128)(2,1)}) custom-call(s32[4096]{0:T(1024)} %bitcast.46, s32[4096]{0:T(1024)} %bitcast.47, s32[2]{0:T(128)} %pad_add_fusion.which, bf16[4096,1536]{1,0:T(8,128)(2,1)} %all-gather.4.cloned.1.call-done.rows_hbm, f32[16,2048]{1,0:T(8,128)} %constant.42.clone.table_ref, ...), custom_call_target="tpu_custom_call" | custom-call | flops 24000000000 | bytes 12000000 | tf_op jit(solution)/shard_map/head/pallas_call | solution.py:367
  114.7 2.1 collective-permute-start.4
  118.1 6.2 %collective-permute-done.4.refs_0_ = bf16[2,24,768]{2,1,0:T(8,128)(2,1)S(1)} collective-permute-done((bf16[2,24,768]{2,1,0:T(8,128)(2,1)S(1)}, bf16[2,24,768]{2,1,0:T(8,128)(2,1)S(1)}, u32[]{:S(2)}, u32[]{:S(2)}) %collective-permute-start.4) | collective-permute-done | bytes 73760 | tf_op jit(solution)/shard_map/rounds/ppermute | solution.py:51
  124.3 4.0 %collective-permute-done.6.refs_2_ = bf16[2,24,768]{2,1,0:T(8,128)(2,1)S(1)} collective-permute-done((bf16[2,24,768]{2,1,0:T(8,128)(2,1)S(1)}, bf16[2,24,768]{2,1,0:T(8,128)(2,1)S(1)}, u32[]{:S(2)}, u32[]{:S(2)}) %collective-permute-start.6) | collective-permute-done | bytes 73760 | tf_op jit(solution)/shard_map/rounds/ppermute | solution.py:51
  129.1 2.2 rounds.5
  131.3 3.3 %collective-permute-start.11 = (bf16[272,768]{1,0:T(8,128)(2,1)}, bf16[272,768]{1,0:T(8,128)(2,1)S(1)}, u32[]{:S(2)}, u32[]{:S(2)}) collective-permute-start(bf16[272,768]{1,0:T(8,128)(2,1)} %get-tuple-element.66.refs_3_), channel_id=1, source_target_pairs={{0,2},{1,3},{2,0},{3,1},{4,6},{5,7},{6,4},{7,5},{8,10},{9,11},{10,... | collective-permute-start | bytes 1253384 | tf_op jit(solution)/shard_map/rounds/ppermute | solution.py:51
  137.4 3.0 %collective-permute-done.10.refs_2_ = bf16[2,96,768]{2,1,0:T(8,128)(2,1)S(1)} collective-permute-done((bf16[2,96,768]{2,1,0:T(8,128)(2,1)}, bf16[2,96,768]{2,1,0:T(8,128)(2,1)S(1)}, u32[]{:S(2)}, u32[]{:S(2)}) %collective-permute-start.10) | collective-permute-done | bytes 294944 | tf_op jit(solution)/shard_map/rounds/ppermute | solution.py:51
  140.4 3.2 %collective-permute-done.8.refs_0_ = bf16[2,96,768]{2,1,0:T(8,128)(2,1)S(1)} collective-permute-done((bf16[2,96,768]{2,1,0:T(8,128)(2,1)}, bf16[2,96,768]{2,1,0:T(8,128)(2,1)S(1)}, u32[]{:S(2)}, u32[]{:S(2)}) %collective-permute-start.8) | collective-permute-done | bytes 294944 | tf_op jit(solution)/shard_map/rounds/ppermute | solution.py:51
  143.6 7.6 %collective-permute-done.9.refs_1_ = bf16[2,96,768]{2,1,0:T(8,128)(2,1)S(1)} collective-permute-done((bf16[2,96,768]{2,1,0:T(8,128)(2,1)}, bf16[2,96,768]{2,1,0:T(8,128)(2,1)S(1)}, u32[]{:S(2)}, u32[]{:S(2)}) %collective-permute-start.9) | collective-permute-done | bytes 294944 | tf_op jit(solution)/shard_map/rounds/ppermute | solution.py:51
  151.2 1.8 collective-permute-done.12.refs_5_
  154.0 3.0 %rounds.6 = (bf16[2,384,768]{2,1,0:T(8,128)(2,1)}, bf16[272,768]{1,0:T(8,128)(2,1)}) custom-call(s32[1]{0:T(128)} %bitcast.11.which, bf16[2,96,768]{2,1,0:T(8,128)(2,1)} %get-tuple-element.65.own_ref, bf16[2,96,768]{2,1,0:T(8,128)(2,1)} %copy-done.14, bf16[2,96,768]{2,1,0:T(8,128)(2,1)} %copy-done.15, bf16[2,96,768]{2,1,0:T(8,128)(2,1)} %copy-done.13, ...), custom_call_target="tpu_custom_call" | custom-call | tf_op jit(solution)/shard_map/rounds/pallas_call | solution.py:515
  157.0 5.5 %collective-permute-start.17 = (bf16[2,384,768]{2,1,0:T(8,128)(2,1)}, bf16[2,384,768]{2,1,0:T(8,128)(2,1)}, u32[]{:S(2)}, u32[]{:S(2)}) collective-permute-start(bf16[2,384,768]{2,1,0:T(8,128)(2,1)} %get-tuple-element.67.refs_0_.mine_ref), channel_id=1, source_target_pairs={{0,8},{1,9},{2,10},{3,11},{4,12},{5,13},{6,14},{7,15},{8,0},{9,1},... | collective-permute-start | bytes 3538952 | tf_op jit(solution)/shard_map/feed_gather/ppermute | solution.py:51
  163.4 4.7 %all-to-all-start.1 = ((bf16[16,256,256]{2,1,0:T(8,128)(2,1)}), bf16[16,256,256]{2,1,0:T(8,128)(2,1)S(1)}, u32[]{:S(2)}, u32[]{:S(2)}) async-start(bf16[16,256,256]{2,1,0:T(8,128)(2,1)} %rounds.7), calls=%async_computation.1 | async-start | bytes 4194304 | tf_op jit(solution)/shard_map/rounds/all_to_all | solution.py:839
  168.6 4.8 %feed_gather.6 = (f32[3072,768]{1,0:T(8,128)}, f32[768,3072]{1,0:T(8,128)}) custom-call(s32[2]{0:T(128)} %pad_add_fusion.3.where, bf16[2,384,768]{2,1,0:T(8,128)(2,1)} %get-tuple-element.67.refs_0_.mine_ref, bf16[2,384,768]{2,1,0:T(8,128)(2,1)} %collective-permute-done.17.theirs_ref), custom_call_target="tpu_custom_call" | custom-call | bytes 7000000 | tf_op jit(solution)/shard_map/feed_gather/pallas_call | solution.py:594
  173.4 15.5 %collective-permute-done.16.value_ref = bf16[2,384,768]{2,1,0:T(8,128)(2,1)S(1)} collective-permute-done((bf16[2,384,768]{2,1,0:T(8,128)(2,1)}, bf16[2,384,768]{2,1,0:T(8,128)(2,1)S(1)}, u32[]{:S(2)}, u32[]{:S(2)}) %collective-permute-start.16) | collective-permute-done | bytes 1179680 | tf_op jit(solution)/shard_map/rounds/ppermute | solution.py:51
  190.0 3.3 %collective-permute-start.18 = (bf16[2,384,768]{2,1,0:T(8,128)(2,1)}, bf16[2,384,768]{2,1,0:T(8,128)(2,1)}, u32[]{:S(2)}, u32[]{:S(2)}) collective-permute-start(bf16[2,384,768]{2,1,0:T(8,128)(2,1)} %feed_gather.7.mine_ref), channel_id=1, source_target_pairs={{0,8},{1,9},{2,10},{3,11},{4,12},{5,13},{6,14},{7,15},{8,0},{9,1},... | collective-permute-start | bytes 3538952 | tf_op jit(solution)/shard_map/feed_gather/ppermute | solution.py:51
  196.1 4.8 %feed_gather.8 = (f32[3072,768]{1,0:T(8,128)}, f32[768,3072]{1,0:T(8,128)}) custom-call(s32[2]{0:T(128)} %pad_add_fusion.2.where, bf16[2,384,768]{2,1,0:T(8,128)(2,1)} %feed_gather.7.mine_ref, bf16[2,384,768]{2,1,0:T(8,128)(2,1)} %collective-permute-done.18.theirs_ref, ...), custom_call_target="tpu_custom_call", output_to_operand_aliasing={{0}: (3, {}), {1}: (4, {})} | custom-call | bytes 7000000 | tf_op jit(solution)/shard_map/feed_gather/pallas_call | solution.py:594
  200.9 4.8 %feed_gather.9 = (f32[3072,768]{1,0:T(8,128)}, f32[768,3072]{1,0:T(8,128)}) custom-call(s32[2]{0:T(128)} %pad_add_fusion.1.where, bf16[2,384,768]{2,1,0:T(8,128)(2,1)} %collective-permute-done.14.mine_ref, bf16[2,384,768]{2,1,0:T(8,128)(2,1)} %collective-permute-done.15.theirs_ref, ...), custom_call_target="tpu_custom_call", output_to_operand_aliasing={{0}: (3, {}), {1}: (4, {})} | custom-call | bytes 7000000 | tf_op jit(solution)/shard_map/feed_gather/pallas_call | solution.py:594
  205.7 8.9 %all-to-all-done.1.value_ref = bf16[16,256,256]{2,1,0:T(8,128)(2,1)S(1)} async-done(((bf16[16,256,256]{2,1,0:T(8,128)(2,1)}), bf16[16,256,256]{2,1,0:T(8,128)(2,1)S(1)}, u32[]{:S(2)}, u32[]{:S(2)}) %all-to-all-start.1) | async-done | bytes 2097184 | tf_op jit(solution)/shard_map/rounds/all_to_all | solution.py:839
  216.4 6.7 %heads_back.3 = (bf16[256,768]{1,0:T(8,128)(2,1)}, f32[256,768]{1,0:T(8,128)}) custom-call(bf16[16,256,256]{2,1,0:T(8,128)(2,1)} %heads_back.2.back_ref, bf16[256,768]{1,0:T(8,128)(2,1)} %bitcast.42, bf16[256,768]{1,0:T(8,128)(2,1)} %bitcast.38, f32[256,768]{1,0:T(8,128)} %get-tuple-element.57.normal_ref, f32[256,128]{1,0:T(8,128)} %get-tuple-element.73.rate_ref, ...), custom_call_target="tpu_custom_call" | custom-call | tf_op jit(solution)/shard_map/feed_gather/heads_back/pallas_call | solution.py:708
  223.7 2.4 collective-permute-done.20.theirs_ref
  227.2 4.8 %feed_gather.11 = (f32[3072,768]{1,0:T(8,128)}, f32[768,3072]{1,0:T(8,128)}) custom-call(s32[2]{0:T(128)} %pad_add_fusion.4.where, bf16[2,384,768]{2,1,0:T(8,128)(2,1)} %feed_gather.10.mine_ref, bf16[2,384,768]{2,1,0:T(8,128)(2,1)} %copy-done.8, f32[3072,768]{1,0:T(8,128)} %get-tuple-element.72.refs_0_, ...), custom_call_target="tpu_custom_call", output_to_operand_aliasing={{0}: (3, {}), {1}: (4, {})} | custom-call | bytes 7000000 | tf_op jit(solution)/shard_map/feed_gather/pallas_call | solution.py:594
  231.9 7.8 %head_place.1 = (f32[768,2304]{1,0:T(8,128)}, f32[768,768]{1,0:T(8,128)}, f32[768]{0:T(1024)}, f32[768]{0:T(1024)}, f32[2304]{0:T(1024)}, /*index=5*/f32[768]{0:...) custom-call(bf16[16,272,768]{2,1,0:T(8,128)(2,1)} %bitcast.34, bf16[16,272,768]{2,1,0:T(8,128)(2,1)} %bitcast.35), custom_call_target="tpu_custom_call" | custom-call | tf_op jit(solution)/shard_map/head_place/pallas_call | solution.py:649
  (114 shorter events, 31.9 us)
Async XLA Ops:
  7.2 76.8 %all-gather.4.cloned.1.call-start = ((), (), s32[]{:S(2)}) async-start(), calls=%async_computation.2 | async-start | bytes 13369344 | tf_op jit(solution)/shard_map/gather_rows/all_gather | solution.py:758
  10.2 2.9 %collective-permute-start = (bf16[256,1536]{1,0:T(8,128)(2,1)}, bf16[256,1536]{1,0:T(8,128)(2,1)S(1)}, u32[]{:S(2)}, u32[]{:S(2)}) collective-permute-start(bf16[256,1536]{1,0:T(8,128)(2,1)} %get-tuple-element.53.own_ref), channel_id=1, source_target_pairs={{0,8},{1,9},{2,10},{3,11},{4,12},{5,13},{6,14},{7,15},{8,0},{9,1},... | collective-permute-start | bytes 2359304 | tf_op jit(solution)/shard_map/feed/ppermute | solution.py:51
  14.0 12.2 %copy-start.20 = (bf16[768]{0:T(1024)(128)(2,1)S(1)}, bf16[768]{0:T(1024)(128)(2,1)}, u32[]{:S(2)}) copy-start(bf16[768]{0:T(1024)(128)(2,1)} %gain1_ref.3) | copy-start | bytes 4612
  14.0 12.2 %copy-start.24 = (bf16[768]{0:T(1024)(128)(2,1)S(1)}, bf16[768]{0:T(1024)(128)(2,1)}, u32[]{:S(2)}) copy-start(bf16[768]{0:T(1024)(128)(2,1)} %shift1_ref.1) | copy-start | bytes 4612
  23.6 29.2 %collective-permute-start.2 = (bf16[2,768,768]{2,1,0:T(8,128)(2,1)}, bf16[2,768,768]{2,1,0:T(8,128)(2,1)S(1)}, u32[]{:S(2)}, u32[]{:S(2)}) collective-permute-start(bf16[2,768,768]{2,1,0:T(8,128)(2,1)} %get-tuple-element.61), channel_id=1, source_target_pairs={{0,2},{1,3},{2,0},{3,1},{4,6},{5,7},{6,4},{7,5},{8,14},{9,15},{10,... | collective-permute-start | bytes 7077896 | tf_op jit(solution)/shard_map/feed_scatter/ppermute | solution.py:51
  36.9 23.9 %collective-permute-start.1 = (bf16[256,1536]{1,0:T(8,128)(2,1)}, bf16[256,1536]{1,0:T(8,128)(2,1)}, u32[]{:S(2)}, u32[]{:S(2)}) collective-permute-start(bf16[256,1536]{1,0:T(8,128)(2,1)} %get-tuple-element.56), channel_id=1, source_target_pairs={{0,8},{1,9},{2,10},{3,11},{4,12},{5,13},{6,14},{7,15},{8,0},{9,1},... | collective-permute-start | bytes 2359304 | tf_op jit(solution)/shard_map/feed/ppermute | solution.py:51
  58.5 5.4 %copy-start.5 = (f32[256,768]{1,0:T(8,128)S(1)}, f32[256,768]{1,0:T(8,128)}, u32[]{:S(2)}) copy-start(f32[256,768]{1,0:T(8,128)} %get-tuple-element.57.normal_ref) | copy-start | bytes 2359300
  58.5 15.7 %collective-permute-start.3 = (bf16[2,384,768]{2,1,0:T(8,128)(2,1)}, bf16[2,384,768]{2,1,0:T(8,128)(2,1)}, u32[]{:S(2)}, u32[]{:S(2)}) collective-permute-start(bf16[2,384,768]{2,1,0:T(8,128)(2,1)} %constant_dynamic-slice_fusion), channel_id=1, source_target_pairs={{0,6},{1,7},{2,4},{3,5},{4,2},{5,3},{6,0},{7,1},{8,10},{9,11},{10,... | collective-permute-start | bytes 3538952 | tf_op jit(solution)/shard_map/feed_scatter/ppermute | solution.py:51
  76.8 34.4 %all-to-all-start = ((bf16[16,2,24,768]{3,2,1,0:T(8,128)(2,1)}), bf16[16,2,24,768]{3,2,1,0:T(8,128)(2,1)S(1)}, u32[]{:S(2)}, u32[]{:S(2)}) async-start(bf16[16,2,24,768]{3,2,1,0:T(8,128)(2,1)} %bitcast.33), calls=%async_computation | async-start | bytes 2359296 | tf_op jit(solution)/shard_map/feed_scatter/all_to_all | solution.py:787
  83.4 148.6 %all-gather.6.cloned.1.call-start = ((), (), s32[]{:S(2)}) async-start(), calls=%async_computation.3 | async-start | bytes 7102464 | tf_op jit(solution)/shard_map/rounds/all_gather | solution.py:842
  112.3 16.1 %collective-permute-start.7 = (bf16[272,768]{1,0:T(8,128)(2,1)}, bf16[272,768]{1,0:T(8,128)(2,1)S(1)}, u32[]{:S(2)}, u32[]{:S(2)}) collective-permute-start(bf16[272,768]{1,0:T(8,128)(2,1)} %rounds.4.refs_3_), channel_id=1, source_target_pairs={{0,1},{1,0},{2,3},{3,2},{4,5},{5,4},{6,7},{7,6},{8,9},{9,8},{10,11... | collective-permute-start | bytes 1253384 | tf_op jit(solution)/shard_map/rounds/ppermute | solution.py:51
  114.7 13.6 %copy-start.16 = (bf16[2,24,768]{2,1,0:T(8,128)(2,1)}, bf16[2,24,768]{2,1,0:T(8,128)(2,1)S(1)}, u32[]{:S(2)}) copy-start(bf16[2,24,768]{2,1,0:T(8,128)(2,1)S(1)} %fusion.own_ref) | copy-start | bytes 221188
  114.7 9.6 %collective-permute-start.4 = (bf16[2,24,768]{2,1,0:T(8,128)(2,1)S(1)}, bf16[2,24,768]{2,1,0:T(8,128)(2,1)S(1)}, u32[]{:S(2)}, u32[]{:S(2)}) collective-permute-start(bf16[2,24,768]{2,1,0:T(8,128)(2,1)S(1)} %fusion.own_ref), channel_id=1, source_target_pairs={{0,1},{1,0},{2,3},{3,2},{4,5},{5,4},{6,7},{7,6},{8,9},{9,8},{10,11... | collective-permute-start | bytes 221192 | tf_op jit(solution)/shard_map/rounds/ppermute | solution.py:51
  116.8 7.5 %collective-permute-start.5 = (bf16[2,24,768]{2,1,0:T(8,128)(2,1)S(1)}, bf16[2,24,768]{2,1,0:T(8,128)(2,1)S(1)}, u32[]{:S(2)}, u32[]{:S(2)}) collective-permute-start(bf16[2,24,768]{2,1,0:T(8,128)(2,1)S(1)} %fusion.own_ref), channel_id=1, source_target_pairs={{0,16},{1,17},{2,18},{3,19},{4,20},{5,21},{6,22},{7,23},{8,24},{9,... | collective-permute-start | bytes 221192 | tf_op jit(solution)/shard_map/rounds/ppermute | solution.py:51
  117.2 11.2 %collective-permute-start.6 = (bf16[2,24,768]{2,1,0:T(8,128)(2,1)S(1)}, bf16[2,24,768]{2,1,0:T(8,128)(2,1)S(1)}, u32[]{:S(2)}, u32[]{:S(2)}) collective-permute-start(bf16[2,24,768]{2,1,0:T(8,128)(2,1)S(1)} %fusion.own_ref), channel_id=1, source_target_pairs={{0,17},{1,16},{2,19},{3,18},{4,21},{5,20},{6,23},{7,22},{8,25},{9,... | collective-permute-start | bytes 221192 | tf_op jit(solution)/shard_map/rounds/ppermute | solution.py:51
  124.3 4.0 %copy-start.18 = (bf16[2,24,768]{2,1,0:T(8,128)(2,1)}, bf16[2,24,768]{2,1,0:T(8,128)(2,1)S(1)}, u32[]{:S(2)}) copy-start(bf16[2,24,768]{2,1,0:T(8,128)(2,1)S(1)} %collective-permute-done.5.refs_1_) | copy-start | bytes 221188
  131.3 9.1 %collective-permute-start.10 = (bf16[2,96,768]{2,1,0:T(8,128)(2,1)}, bf16[2,96,768]{2,1,0:T(8,128)(2,1)S(1)}, u32[]{:S(2)}, u32[]{:S(2)}) collective-permute-start(bf16[2,96,768]{2,1,0:T(8,128)(2,1)} %get-tuple-element.65.own_ref), channel_id=1, source_target_pairs={{0,96},{1,97},{2,98},{3,99},{4,100},{5,101},{6,102},{7,103},{8,104... | collective-permute-start | bytes 884744 | tf_op jit(solution)/shard_map/rounds/ppermute | solution.py:51
  131.3 19.9 %collective-permute-start.11 = (bf16[272,768]{1,0:T(8,128)(2,1)}, bf16[272,768]{1,0:T(8,128)(2,1)S(1)}, u32[]{:S(2)}, u32[]{:S(2)}) collective-permute-start(bf16[272,768]{1,0:T(8,128)(2,1)} %get-tuple-element.66.refs_3_), channel_id=1, source_target_pairs={{0,2},{1,3},{2,0},{3,1},{4,6},{5,7},{6,4},{7,5},{8,10},{9,11},{10,... | collective-permute-start | bytes 1253384 | tf_op jit(solution)/shard_map/rounds/ppermute | solution.py:51
  134.6 18.4 %collective-permute-start.12 = (bf16[272,768]{1,0:T(8,128)(2,1)}, bf16[272,768]{1,0:T(8,128)(2,1)S(1)}, u32[]{:S(2)}, u32[]{:S(2)}) collective-permute-start(bf16[272,768]{1,0:T(8,128)(2,1)} %get-tuple-element.66.refs_3_), channel_id=1, source_target_pairs={{0,4},{1,5},{2,6},{3,7},{4,0},{5,1},{6,2},{7,3},{8,12},{9,13},{10,... | collective-permute-start | bytes 1253384 | tf_op jit(solution)/shard_map/rounds/ppermute | solution.py:51
  136.1 16.9 %collective-permute-start.13 = (bf16[272,768]{1,0:T(8,128)(2,1)}, bf16[272,768]{1,0:T(8,128)(2,1)S(1)}, u32[]{:S(2)}, u32[]{:S(2)}) collective-permute-start(bf16[272,768]{1,0:T(8,128)(2,1)} %get-tuple-element.66.refs_3_), channel_id=1, source_target_pairs={{0,6},{1,7},{2,4},{3,5},{4,2},{5,3},{6,0},{7,1},{8,14},{9,15},{10,... | collective-permute-start | bytes 1253384 | tf_op jit(solution)/shard_map/rounds/ppermute | solution.py:51
  137.0 6.6 %collective-permute-start.8 = (bf16[2,96,768]{2,1,0:T(8,128)(2,1)}, bf16[2,96,768]{2,1,0:T(8,128)(2,1)S(1)}, u32[]{:S(2)}, u32[]{:S(2)}) collective-permute-start(bf16[2,96,768]{2,1,0:T(8,128)(2,1)} %get-tuple-element.65.own_ref), channel_id=1, source_target_pairs={{0,32},{1,33},{2,34},{3,35},{4,36},{5,37},{6,38},{7,39},{8,40},{9,... | collective-permute-start | bytes 884744 | tf_op jit(solution)/shard_map/rounds/ppermute | solution.py:51
  140.4 12.6 %copy-start.13 = (bf16[2,96,768]{2,1,0:T(8,128)(2,1)}, bf16[2,96,768]{2,1,0:T(8,128)(2,1)S(1)}, u32[]{:S(2)}) copy-start(bf16[2,96,768]{2,1,0:T(8,128)(2,1)S(1)} %collective-permute-done.10.refs_2_) | copy-start | bytes 884740
  140.4 10.8 %collective-permute-start.9 = (bf16[2,96,768]{2,1,0:T(8,128)(2,1)}, bf16[2,96,768]{2,1,0:T(8,128)(2,1)S(1)}, u32[]{:S(2)}, u32[]{:S(2)}) collective-permute-start(bf16[2,96,768]{2,1,0:T(8,128)(2,1)} %get-tuple-element.65.own_ref), channel_id=1, source_target_pairs={{0,64},{1,65},{2,66},{3,67},{4,68},{5,69},{6,70},{7,71},{8,72},{9,... | collective-permute-start | bytes 884744 | tf_op jit(solution)/shard_map/rounds/ppermute | solution.py:51
  143.6 9.4 %copy-start.14 = (bf16[2,96,768]{2,1,0:T(8,128)(2,1)}, bf16[2,96,768]{2,1,0:T(8,128)(2,1)S(1)}, u32[]{:S(2)}) copy-start(bf16[2,96,768]{2,1,0:T(8,128)(2,1)S(1)} %collective-permute-done.8.refs_0_) | copy-start | bytes 884740
  157.0 11.6 %collective-permute-start.17 = (bf16[2,384,768]{2,1,0:T(8,128)(2,1)}, bf16[2,384,768]{2,1,0:T(8,128)(2,1)}, u32[]{:S(2)}, u32[]{:S(2)}) collective-permute-start(bf16[2,384,768]{2,1,0:T(8,128)(2,1)} %get-tuple-element.67.refs_0_.mine_ref), channel_id=1, source_target_pairs={{0,8},{1,9},{2,10},{3,11},{4,12},{5,13},{6,14},{7,15},{8,0},{9,1},... | collective-permute-start | bytes 3538952 | tf_op jit(solution)/shard_map/feed_gather/ppermute | solution.py:51
  162.5 26.5 %collective-permute-start.16 = (bf16[2,384,768]{2,1,0:T(8,128)(2,1)}, bf16[2,384,768]{2,1,0:T(8,128)(2,1)S(1)}, u32[]{:S(2)}, u32[]{:S(2)}) collective-permute-start(bf16[2,384,768]{2,1,0:T(8,128)(2,1)} %get-tuple-element.67.refs_0_.mine_ref), channel_id=1, source_target_pairs={{0,6},{1,7},{2,4},{3,5},{4,2},{5,3},{6,0},{7,1},{8,10},{9,11},{10,... | collective-permute-start | bytes 3538952 | tf_op jit(solution)/shard_map/rounds/ppermute | solution.py:51
  162.5 30.8 %collective-permute-start.14 = (bf16[2,384,768]{2,1,0:T(8,128)(2,1)}, bf16[2,384,768]{2,1,0:T(8,128)(2,1)}, u32[]{:S(2)}, u32[]{:S(2)}) collective-permute-start(bf16[2,384,768]{2,1,0:T(8,128)(2,1)} %get-tuple-element.67.refs_0_.mine_ref), channel_id=1, source_target_pairs={{0,2},{1,3},{2,0},{3,1},{4,6},{5,7},{6,4},{7,5},{8,14},{9,15},{10,... | collective-permute-start | bytes 3538952 | tf_op jit(solution)/shard_map/rounds/ppermute | solution.py:51
  163.4 51.2 %all-to-all-start.1 = ((bf16[16,256,256]{2,1,0:T(8,128)(2,1)}), bf16[16,256,256]{2,1,0:T(8,128)(2,1)S(1)}, u32[]{:S(2)}, u32[]{:S(2)}) async-start(bf16[16,256,256]{2,1,0:T(8,128)(2,1)} %rounds.7), calls=%async_computation.1 | async-start | bytes 4194304 | tf_op jit(solution)/shard_map/rounds/all_to_all | solution.py:839
  190.0 6.1 %collective-permute-start.18 = (bf16[2,384,768]{2,1,0:T(8,128)(2,1)}, bf16[2,384,768]{2,1,0:T(8,128)(2,1)}, u32[]{:S(2)}, u32[]{:S(2)}) collective-permute-start(bf16[2,384,768]{2,1,0:T(8,128)(2,1)} %feed_gather.7.mine_ref), channel_id=1, source_target_pairs={{0,8},{1,9},{2,10},{3,11},{4,12},{5,13},{6,14},{7,15},{8,0},{9,1},... | collective-permute-start | bytes 3538952 | tf_op jit(solution)/shard_map/feed_gather/ppermute | solution.py:51
  193.3 7.6 %collective-permute-start.15 = (bf16[2,384,768]{2,1,0:T(8,128)(2,1)}, bf16[2,384,768]{2,1,0:T(8,128)(2,1)}, u32[]{:S(2)}, u32[]{:S(2)}) collective-permute-start(bf16[2,384,768]{2,1,0:T(8,128)(2,1)} %collective-permute-done.14.mine_ref), channel_id=1, source_target_pairs={{0,8},{1,9},{2,10},{3,11},{4,12},{5,13},{6,14},{7,15},{8,0},{9,1},... | collective-permute-start | bytes 3538952 | tf_op jit(solution)/shard_map/feed_gather/ppermute | solution.py:51
  193.3 21.3 %collective-permute-start.19 = (bf16[2,384,768]{2,1,0:T(8,128)(2,1)}, bf16[2,384,768]{2,1,0:T(8,128)(2,1)S(1)}, u32[]{:S(2)}, u32[]{:S(2)}) collective-permute-start(bf16[2,384,768]{2,1,0:T(8,128)(2,1)} %feed_gather.7.mine_ref), channel_id=1, source_target_pairs={{0,2},{1,3},{2,0},{3,1},{4,6},{5,7},{6,4},{7,5},{8,14},{9,15},{10,... | collective-permute-start | bytes 3538952 | tf_op jit(solution)/shard_map/feed_gather/ppermute | solution.py:51
  223.1 3.1 %collective-permute-start.20 = (bf16[2,384,768]{2,1,0:T(8,128)(2,1)}, bf16[2,384,768]{2,1,0:T(8,128)(2,1)S(1)}, u32[]{:S(2)}, u32[]{:S(2)}) collective-permute-start(bf16[2,384,768]{2,1,0:T(8,128)(2,1)} %feed_gather.10.mine_ref), channel_id=1, source_target_pairs={{0,8},{1,9},{2,10},{3,11},{4,12},{5,13},{6,14},{7,15},{8,0},{9,1},... | collective-permute-start | bytes 3538952 | tf_op jit(solution)/shard_map/feed_gather/ppermute | solution.py:51
  (19 other events, 31.1 us)
Sparse Core Ops, SparseCore 0:
  10.4 73.5 all-gather.3
  157.1 70.9 all-gather.5
